TPU v7x, 256 devices: a whole 4x4x8 slice. The times are simulated.
256 devices in a mesh: dp: 32 (over x, z), tensor: 8 (over y, core).
Axes of the slice: x: 4, y: 4, z: 8, core: 2. Of those that a mesh axis runs over, the one named last changes fastest.
Arguments:
- train_acts: bfloat16 [128, 256, 14336], P('dp', None, 'tensor'), may hold values from -16 to 16
- train_grads: bfloat16 [128, 256, 4096], P('dp', None, 'tensor'), may hold values from -16 to 16
- query_acts: bfloat16 [128, 256, 14336], P('dp', None, 'tensor'), may hold values from -16 to 16
- query_grads: bfloat16 [128, 256, 4096], P('dp', None, 'tensor'), may hold values from -16 to 16
- proj_in: bfloat16 [64, 14336], P(None, 'tensor'), may hold values from -0.046875 to 0.046875
- proj_out: bfloat16 [64, 4096], P(None, 'tensor'), may hold values from -0.09375 to 0.09375
Outputs:
- scores: float32 [128, 128], P('dp')
All inputs are finite; a program needn't handle non-finite values.
Results may differ from a plain program's by a relative error of at most 0.0003.
Values sent between devices are 32-bit elements; how exact they have to be, the bound alone decides.
No kernel may reach another device: no remote copies, remote signals or barrier semaphores. Data moves between devices by JAX's collectives and lax.ppermute only.
A program may use at most 64 MiB of HBM per device.

v0:
```python
import jax
import jax.numpy as jnp
from jax import lax
from jax.sharding import PartitionSpec as P

damping = 0.1


def features(acts, grads, proj_in, proj_out):
    rows_in = acts.reshape(-1, acts.shape[-1])
    rows_out = grads.reshape(-1, grads.shape[-1])
    feat_in = lax.dot_general(
        rows_in, proj_in, (((1,), (1,)), ((), ())), preferred_element_type=jnp.float32
    )
    feat_out = lax.dot_general(
        rows_out, proj_out, (((1,), (1,)), ((), ())), preferred_element_type=jnp.float32
    )
    joined = jnp.concatenate([feat_in, feat_out], axis=1)
    return joined.reshape(acts.shape[0], acts.shape[1], joined.shape[1])


def seq_grads(joined, width):
    return jnp.einsum(
        "sto,sti->soi", joined[..., width:], joined[..., :width], precision=lax.Precision.HIGHEST
    )


def factor_terms(joined, width):
    flat = joined.reshape(-1, joined.shape[-1])
    side_in = flat[:, :width]
    side_out = flat[:, width:]
    term_in = lax.dot_general(
        side_in, side_in, (((0,), (0,)), ((), ())), precision=lax.Precision.HIGHEST
    )
    term_out = lax.dot_general(
        side_out, side_out, (((0,), (0,)), ((), ())), precision=lax.Precision.HIGHEST
    )
    return (term_in, term_out)


def precondition(grads, lower_in, lower_out):

    def single(grad):
        left = jax.scipy.linalg.cho_solve((lower_out, True), grad)
        return jax.scipy.linalg.cho_solve((lower_in, True), left.T).T

    return jax.vmap(single)(grads)


def on_device(train_acts, train_grads, query_acts, query_grads, proj_in, proj_out):
    width = proj_in.shape[0]
    seq_len = train_acts.shape[1]
    total = train_acts.shape[0] * seq_len * lax.axis_size("dp")
    train_part = features(train_acts, train_grads, proj_in, proj_out)
    query_part = features(query_acts, query_grads, proj_in, proj_out)
    train_feat, query_feat = lax.psum((train_part, query_part), "tensor")
    term_in, term_out = factor_terms(train_feat, width)
    sum_in, sum_out = lax.psum((term_in, term_out), "dp")
    train_grad = seq_grads(train_feat, width)
    query_grad = seq_grads(query_feat, width)
    identity = jnp.eye(width, dtype=jnp.float32)
    lower_in = jnp.linalg.cholesky(sum_in / total + damping * identity)
    lower_out = jnp.linalg.cholesky(sum_out / total + damping * identity)
    ready = precondition(query_grad, lower_in, lower_out)
    every_query = lax.all_gather(ready, "dp", axis=0, tiled=True)
    scores = jnp.einsum("toi,qoi->tq", train_grad, every_query, precision=lax.Precision.HIGHEST)
    return scores / (seq_len * width)


def solution(mesh):
    placed = (
        P("dp", None, "tensor"),
        P("dp", None, "tensor"),
        P("dp", None, "tensor"),
        P("dp", None, "tensor"),
        P(None, "tensor"),
        P(None, "tensor"),
    )
    return jax.shard_map(
        on_device, mesh=mesh, in_specs=placed, out_specs=P("dp", None), check_vma=False
    )
```

profile of v0, /device:TPU:1, one launch (start us, length us, event | category | flops | bytes accessed | tf_op | source)
XLA Modules:
  0.0 348.9 jit_solution(2647153884059807799)
XLA Ops:
  6.5 0.0 copy-start
  6.5 0.0 all-reduce.4.cloned.1.call-start
  6.5 3.4 fusion.20
  10.0 0.0 copy-start.5
  10.0 0.0 copy-done.4
  10.0 0.0 copy-done.1
  10.0 0.0 copy-start.3
  10.0 1.2 fusion.22
  11.2 0.0 copy-done
  11.2 0.0 copy-done.5
  11.2 0.4 fusion.21
  11.7 0.0 copy-done.3
  11.7 0.4 fusion.23
  12.2 1.1 copy_bitcast_fusion
  13.3 0.0 all-reduce.4.cloned.1.call-update
  13.3 0.0 all-gather.2.cloned.1.call-start
  13.4 69.6 %all-reduce.4.cloned.1.call-done = (f32[4,256,128]{1,2,0:T(8,128)}, f32[4,256,128]{1,2,0:T(8,128)}) async-done(((f32[4,256,128]{1,2,0:T(8,128)}, f32[4,256,128]{1,2,0:T(8,128)}), (f32[4,256,128]{1,2,0:T(8,128)}, f32[4,256,128]{1,2,0:T(8,128)})) %all-reduce.4.cloned.1.call-update) | async-done | bytes 1048592 | tf_op jit(solution)/shard_map/psum | solution.py:56
  83.0 1.3 copy.39
  84.3 1.3 fusion.1
  85.7 1.0 fusion.3
  86.7 1.4 convolution_bitcast_fusion
  88.1 0.1 copy.45
  88.2 115.5 %all-reduce = (f32[64,64]{0,1:T(8,128)S(1)}, f32[64,64]{0,1:T(8,128)S(1)}) all-reduce(f32[64,64]{0,1:T(8,128)S(1)} %fusion.1, f32[64,64]{0,1:T(8,128)S(1)} %fusion.3), channel_id=1, replica_groups=mesh['dp'=32,'tensor'=8] {'dp'}, use_global_device_ids=true, to_apply=%region_4.6 | all-reduce | flops 8192 | bytes 65536 | tf_op jit(solution)/shard_map/psum | solution.py:58
  203.7 0.1 copy.43
  203.8 5.8 %cholesky.55 = f32[64,64]{1,0:T(8,128)S(1)} custom-call(f32[64,64]{1,0:T(8,128)S(1)} %fusion.16), custom_call_target="Cholesky" | custom-call | tf_op jit(solution)/shard_map/jit(cholesky)/cholesky | solution.py:63
  209.7 0.6 compare_reduce_fusion
  210.3 0.7 fusion.13
  211.0 4.9 %custom-call.8 = f32[1,64,64]{1,2,0:T(8,128)S(1)} custom-call(f32[1,64,64]{2,1,0:T(8,128)S(1)} %fusion.13), custom_call_target="InvertDiagBlocksLowerTriangular" | custom-call | tf_op jit(solution)/shard_map/vmap(jit(_cho_solve))/triangular_solve | solution.py:44
  215.9 0.1 copy.41
  216.0 5.8 %cholesky.44 = f32[64,64]{1,0:T(8,128)S(1)} custom-call(f32[64,64]{1,0:T(8,128)S(1)} %fusion.19), custom_call_target="Cholesky" | custom-call | tf_op jit(solution)/shard_map/jit(cholesky)/cholesky | solution.py:62
  221.9 0.6 compare_reduce_fusion.1
  222.6 0.7 fusion.12
  223.2 4.9 %custom-call.9 = f32[1,64,64]{1,2,0:T(8,128)S(1)} custom-call(f32[1,64,64]{2,1,0:T(8,128)S(1)} %fusion.12), custom_call_target="InvertDiagBlocksLowerTriangular" | custom-call | tf_op jit(solution)/shard_map/vmap(jit(_cho_solve))/triangular_solve | solution.py:45
  228.1 0.3 convolution_bitcast_fusion.4
  228.4 0.1 copy.46
  228.5 0.5 convolution_bitcast_fusion.2
  229.0 0.1 copy.48
  229.1 0.3 convolution_bitcast_fusion.3
  229.4 0.1 copy.49
  229.5 0.5 convolution_bitcast_fusion.1
  230.0 0.8 copy.51
  230.8 0.0 all-gather.2.cloned.1.call-update
  230.8 0.0 copy-done.2
  230.8 0.4 fusion.7
  231.2 0.1 copy.52
  231.3 99.5 %all-gather.2.cloned.1.call-done = f32[128,64,64]{2,1,0:T(8,128)} async-done(((f32[4,64,64]{2,1,0:T(8,128)}), f32[128,64,64]{2,1,0:T(8,128)}) %all-gather.2.cloned.1.call-update) | async-done | bytes 2097168 | tf_op jit(solution)/shard_map/all_gather | solution.py:65
  330.8 5.7 %copy.53 = f32[128,64,64]{1,0,2:T(8,128)} copy(f32[128,64,64]{2,1,0:T(8,128)} %all-gather.2.cloned.1.call-done) | data formatting | bytes 4194304 | tf_op jit(solution)/shard_map/all_gather | solution.py:65
  336.4 5.7 %fusion = f32[4,128]{1,0:T(4,128)} fusion(f32[4,64,64]{1,0,2:T(4,128)S(1)} %copy.52, f32[128,64,64]{1,0,2:T(8,128)} %copy.53), kind=kOutput, calls=%fused_computation.6 | convolution fusion | flops 25166336 | bytes 2164736 | tf_op jit(solution)/shard_map/toi,qoi->tq/dot_general | solution.py:66
  (11 shorter events, 0.2 us)
Async XLA Ops:
  6.5 4.7 %copy-start = (bf16[4,256,512]{2,1,0:T(8,128)(2,1)S(1)}, bf16[4,256,512]{2,1,0:T(8,128)(2,1)}, u32[]{:S(2)}) copy-start(bf16[4,256,512]{2,1,0:T(8,128)(2,1)} %param.10) | copy-start | bytes 3145732
  6.5 3.4 copy-start.4
  6.5 76.5 %all-reduce.4.cloned.1.call-start = ((), (), s32[]{:S(2)}) async-start(), calls=%async_computation.1 | async-start | bytes 2097152 | tf_op jit(solution)/shard_map/psum | solution.py:56
  6.5 3.4 copy-start.1
  10.0 1.3 copy-start.5
  10.0 1.7 copy-start.3
  13.3 317.5 %all-gather.2.cloned.1.call-start = ((), (), s32[]{:S(2)}) async-start(), calls=%async_computation | async-start | bytes 4325376 | tf_op jit(solution)/shard_map/all_gather | solution.py:65
  83.0 147.8 %copy-start.2 = (f32[4,256,128]{1,2,0:T(8,128)S(1)}, f32[4,256,128]{1,2,0:T(8,128)}, u32[]{:S(2)}) copy-start(f32[4,256,128]{1,2,0:T(8,128)} %get-tuple-element.9) | copy-start | bytes 1572868
Sparse Core Ops, SparseCore 0:
  13.4 69.5 all-reduce.3
  230.9 99.7 all-gather.1
where the time goes:
time: 351 us; the launch traced here: 349 us
  waiting for transfers between devices  169 us (48%)
  blocking collectives  115 us (33%)
  other arithmetic  24.3 us (7%)
  matrix products  16.9 us (5%)
  between operations  13.6 us (4%)
  local copies, waits for them, and re-layouts  9.47 us (3%)
    psum x1, blocking collectives, on_device(): sum_in, sum_out = lax.psum((term_in, term_out), 'dp')  115 us
    all_gather x1, waiting for transfers between devices, on_device(): every_query = lax.all_gather(ready, 'dp', axis=0, tiled=True)  99.5 us
    psum x1, waiting for transfers between devices, on_device(): train_feat, query_feat = lax.psum((train_part, query_part), 'tensor')  69.6 us
  transfers between devices with their start and end apart: 2, of which 2 were waited for; matrix products, arithmetic and copies ran while one was open for 0% of the time, Pallas kernels for 0%

commit v1 on v0

v1 whole, which is shorter than its diff:
```python
import functools

import jax
import jax.numpy as jnp
from jax import lax
from jax.experimental import pallas as pl
from jax.experimental.pallas import tpu as pltpu
from jax.sharding import Mesh
from jax.sharding import PartitionSpec as P

damping = 0.1
RANK = 64
LANES = 128
PANEL = 8
HIGH = lax.Precision.HIGHEST

VM = pl.BlockSpec(memory_space=pltpu.VMEM)
SM = pl.BlockSpec(memory_space=pltpu.SMEM)
PARAMS = pltpu.CompilerParams(vmem_limit_bytes=32 * 1024 * 1024)


def call(body, out, scratch=()):
    def wrapped(*args):
        return pl.pallas_call(
            body,
            out_shape=out,
            in_specs=[SM] + [VM] * (len(args) - 1),
            out_specs=jax.tree.map(lambda _: VM, out),
            scratch_shapes=list(scratch),
            compiler_params=PARAMS,
        )(*args)

    return wrapped


def f32(*shape):
    return jax.ShapeDtypeStruct(shape, jnp.float32)


def iota(shape, dim):
    return lax.broadcasted_iota(jnp.int32, shape, dim)


def pack(wide):
    lane = iota((32, LANES), 1)
    return jnp.where(lane < RANK, wide[:32], pltpu.roll(wide[32:], RANK, 1))


def unpack(packed):
    return jnp.concatenate([packed, pltpu.roll(packed, RANK, 1)], axis=0)


def gram_kernel(place, parts, send, own):
    total = (parts[0] + parts[1]) + (parts[2] + parts[3])
    gram = lax.dot_general(
        total, total, (((0,), (0,)), ((), ())), precision=HIGH, preferred_element_type=jnp.float32
    )
    top = gram[:RANK]
    low = gram[RANK:]
    side_out = pltpu.roll(low, RANK, 1)
    row = iota((RANK, LANES), 0)
    lane = iota((RANK, LANES), 1)
    both = pack(jnp.where(row <= lane, top, side_out))
    diag = jnp.sum(jnp.where(row == lane, side_out, 0.0), axis=0, keepdims=True)
    grad = pack(low)
    own[...] = grad
    is_train = place[3] == 0
    first = jnp.where(is_train, both, grad)
    rest = jnp.broadcast_to(diag, (8, LANES))
    for peer in range(send.shape[0]):
        send[peer, :32] = first
        send[peer, 32:40] = rest


def spread_kernel(place, got, own, send):
    @pl.when(place[3] == 0)
    def _():
        total = got[0]
        for peer in range(1, got.shape[0]):
            total = total + got[peer]
        grad = own[...]
        for peer in range(send.shape[0]):
            send[peer, :40] = total
            send[peer, 40:72] = grad

    @pl.when(place[3] != 0)
    def _():
        for share in range(4):
            for query in range(got.shape[0]):
                tile = got[query, 8 * share : 8 * share + 8]
                for column in range(4):
                    send[column * 4 + share, 8 * query : 8 * query + 8] = tile
        for peer in range(send.shape[0]):
            send[peer, 64:72] = got[0, 32:40]


def invert(wide):
    lane = iota((1, LANES), 1)
    sub = iota((RANK, 1), 0)
    left = lane < RANK
    inner = lane & (RANK - 1)
    for start in range(0, RANK, PANEL):
        columns = [
            jnp.where(
                left,
                jnp.broadcast_to(wide[:, k : k + 1], (RANK, LANES)),
                jnp.broadcast_to(wide[:, RANK + k : RANK + k + 1], (RANK, LANES)),
            )
            for k in range(start, start + PANEL)
        ]
        for step in range(PANEL):
            k = start + step
            column = columns[step]
            inverse = 1.0 / column[k : k + 1]
            here = inner == k
            scaled = jnp.where(here, inverse, wide[k : k + 1] * inverse)
            is_row = sub == k
            wide = jnp.where(is_row, scaled, jnp.where(here, 0.0, wide) - column * scaled)
            for later in range(step + 1, PANEL):
                ratio = columns[later][k : k + 1] * inverse
                columns[later] = jnp.where(is_row, ratio, columns[later] - column * ratio)
    return wide


def ready_kernel(total_tokens, place, got, out, held):
    total = got[0, :40]
    for peer in range(1, got.shape[0]):
        total = total + got[peer, :40]
    both = unpack(total[:32])[:, :RANK]
    flipped = both.T
    diag = total[32:33, :RANK]
    row = iota((RANK, RANK), 0)
    lane = iota((RANK, RANK), 1)
    factor_in = jnp.where(row <= lane, both, flipped)
    factor_out = jnp.where(row > lane, both, jnp.where(row == lane, diag, flipped))
    eye = jnp.where(row == lane, damping, 0.0)
    wide = jnp.concatenate(
        [factor_in * (1.0 / total_tokens) + eye, factor_out * (1.0 / total_tokens) + eye], axis=1
    )
    wide = invert(wide)
    held[...] = pltpu.roll(wide, RANK, 1)
    inverse_in = wide[:, :RANK]
    share = pl.multiple_of(place[2] * 8, 8)
    inverse_out = jnp.concatenate(
        [held[pl.ds(share, 8), :RANK], held[pl.ds(share + 32, 8), :RANK]], axis=0
    )
    lefts = []
    for seq in range(4):
        grad = unpack(got[place[0] * 4 + seq, 40:72])[:, :RANK]
        lefts.append(
            jnp.dot(inverse_out, grad, precision=HIGH, preferred_element_type=jnp.float32)
        )
    ready = jnp.dot(
        jnp.concatenate(lefts, axis=0), inverse_in, precision=HIGH, preferred_element_type=jnp.float32
    )
    ready = jnp.concatenate([ready, ready], axis=1)
    half = iota((8, LANES), 1) < RANK
    for seq in range(4):
        out[8 * seq : 8 * seq + 8] = jnp.where(
            half, ready[16 * seq : 16 * seq + 8], ready[16 * seq + 8 : 16 * seq + 16]
        )


def score_kernel(scale, place, got, ready, send):
    tiles = []
    for x in range(4):
        for z in range(8):
            for y in range(4):
                tiles.append(got[x * 4 + y, 8 * z : 8 * z + 8])
    queries = jnp.concatenate(tiles, axis=0)
    pairs = lax.dot_general(
        queries,
        ready[...],
        (((1,), (1,)), ((), ())),
        precision=HIGH,
        preferred_element_type=jnp.float32,
    )
    count = len(tiles)
    same = (iota((8 * count, 32), 0) & 7) == (iota((8 * count, 32), 1) & 7)
    sums = jnp.where(same, pairs, 0.0).reshape(count, 8, 32).sum(axis=1)
    pick = jnp.where(iota((8, 32), 0) == iota((8, 32), 1) // 8, scale, 0.0)
    scores = lax.dot_general(
        pick, sums, (((1,), (1,)), ((), ())), precision=HIGH, preferred_element_type=jnp.float32
    )
    for peer in range(send.shape[0]):
        send[peer] = scores


def total_kernel(place, got, out):
    total = (got[1] + got[3]) + (got[5] + got[7])
    out[...] = total[:4]


def features(acts, grads, proj_in, proj_out):
    rows_in = acts.reshape(-1, acts.shape[-1])
    rows_out = grads.reshape(-1, grads.shape[-1])
    feat_in = lax.dot_general(
        rows_in, proj_in, (((1,), (1,)), ((), ())), preferred_element_type=jnp.float32
    )
    feat_out = lax.dot_general(
        rows_out, proj_out, (((1,), (1,)), ((), ())), preferred_element_type=jnp.float32
    )
    return jnp.concatenate([feat_in, feat_out], axis=1)


def swap(value, axis):
    return lax.all_to_all(value, axis, 0, 0, tiled=True)


def on_device(train_acts, train_grads, query_acts, query_grads, proj_in, proj_out):
    seq_len = train_acts.shape[1]
    total_tokens = train_acts.shape[0] * seq_len * 32
    place = jnp.stack([lax.axis_index(name) for name in ("x", "z", "y", "c")]).astype(jnp.int32)
    is_train = place[3] == 0
    train = features(train_acts, train_grads, proj_in, proj_out)
    query = features(query_acts, query_grads, proj_in, proj_out)
    other = lax.ppermute(jnp.where(is_train, query, train), "c", [(0, 1), (1, 0)])
    mine = jnp.where(is_train, train, query) + other
    parts = swap(mine.reshape(4, seq_len, LANES), "y")
    send, own = call(gram_kernel, (f32(8, 40, LANES), f32(32, LANES)))(place, parts)
    got = swap(send, "z")
    send = call(spread_kernel, f32(16, 72, LANES))(place, got, own)
    got = swap(send, ("x", "y"))
    ready = call(
        functools.partial(ready_kernel, total_tokens),
        f32(32, LANES),
        [pltpu.VMEM((RANK, LANES), jnp.float32)],
    )(place, got)
    ready = lax.ppermute(ready, "c", [(0, 1), (1, 0)])
    scale = 1.0 / (seq_len * RANK)
    send = call(functools.partial(score_kernel, scale), f32(8, 8, LANES))(place, got, ready)
    return call(total_kernel, f32(4, LANES))(place, swap(send, ("y", "c")))


def solution(mesh):
    split = Mesh(mesh.devices.reshape(4, 8, 4, 2), ("x", "z", "y", "c"))
    dp = ("x", "z")
    tensor = ("y", "c")
    placed = (
        P(dp, None, tensor),
        P(dp, None, tensor),
        P(dp, None, tensor),
        P(dp, None, tensor),
        P(None, tensor),
        P(None, tensor),
    )
    return jax.shard_map(
        on_device, mesh=split, in_specs=placed, out_specs=P(dp, None), check_vma=False
    )
```

time: 351 us -> 73.7 us (0.21)
  waiting for transfers between devices: 169 us -> 11.5 us
  blocking collectives: 115 us -> 36.5 us
  other arithmetic: 24.3 us -> 0.23 us
  between operations: 13.6 us -> 0.14 us
  matrix products: 16.9 us -> 5.48 us
  starting transfers between devices: 0.04 us -> 11.2 us
  local copies, waits for them, and re-layouts: 9.47 us -> 1.02 us
  Pallas kernels: 0 us -> 7.48 us
    psum x1 -> x0, blocking collectives: 115 us -> none  [on_device(): sum_in, sum_out = lax.psum((term_in, term_out), 'dp')]
    all_gather x1 -> x0, waiting for transfers between devices: 99.5 us -> none  [on_device(): every_query = lax.all_gather(ready, 'dp', axis=0, tiled=True)]
    psum x1 -> x0, waiting for transfers between devices: 69.6 us -> none  [on_device(): train_feat, query_feat = lax.psum((train_part, query_part), 'tensor')]
    all_to_all x0 -> x3, blocking collectives: none -> 36.5 us  [swap(): return lax.all_to_all(value, axis, 0, 0, tiled=True)]
    another operation x10 -> x1, other arithmetic: 24.1 us -> 0.08 us  [on_device(): jnp.stack([lax.axis_index(name) for name in ('x', 'z', 'y', 'c')])]
    dot_general x5 -> x0, matrix products: 9.77 us -> none  [the longest x1 5.66 us: on_device(): jnp.einsum('toi,qoi->tq', train_grad, every_query, precision=lax.Precisio...]
    all_to_all x0 -> x1, waiting for transfers between devices: none -> 9.11 us  [swap(): return lax.all_to_all(value, axis, 0, 0, tiled=True)]
    ppermute x0 -> x2, starting transfers between devices: none -> 7.69 us  [the longest x1 4.37 us: on_device(): ready = lax.ppermute(ready, 'c', [(0, 1), (1, 0)])]
  transfers between devices with their start and end apart: 2 -> 3, of which waited for: 2 -> 3; matrix products, arithmetic and copies ran while one was open for 0% -> 0% of each run, Pallas kernels for 0% -> 0%
where the time goes in v1:
time: 73.7 us; the launch traced here: 73.5 us
  blocking collectives  36.5 us (50%)
  waiting for transfers between devices  11.5 us (16%)
  starting transfers between devices  11.2 us (15%)
  Pallas kernels  7.48 us (10%)
  matrix products  5.48 us (7%)
  local copies, waits for them, and re-layouts  1.02 us (1%)
    all_to_all x3, blocking collectives, swap(): return lax.all_to_all(value, axis, 0, 0, tiled=True)  36.5 us
    all_to_all x1, waiting for transfers between devices, swap(): return lax.all_to_all(value, axis, 0, 0, tiled=True)  9.11 us
    pallas_call x5, Pallas kernels, wrapped(): pl.pallas_call(body, out_shape=out, in_specs=[SM] + [VM] * (len(args) - 1...  7.48 us
    dot_general x2, matrix products, features(): lax.dot_general(rows_in, proj_in, (((1,), (1,)), ((), ())), preferred_ele...  4.61 us
    ppermute x1, starting transfers between devices, on_device(): ready = lax.ppermute(ready, 'c', [(0, 1), (1, 0)])  4.37 us
    all_to_all x1, starting transfers between devices, swap(): return lax.all_to_all(value, axis, 0, 0, tiled=True)  3.47 us
    ppermute x1, starting transfers between devices, on_device(): lax.ppermute(jnp.where(is_train, query, train), 'c', [(0, 1), (1, 0)])  3.32 us
    ppermute x1, waiting for transfers between devices, on_device(): lax.ppermute(jnp.where(is_train, query, train), 'c', [(0, 1), (1, 0)])  1.54 us
  transfers between devices with their start and end apart: 3, of which 3 were waited for; matrix products, arithmetic and copies ran while one was open for 0% of the time, Pallas kernels for 0%

profile of v1, /device:TPU:1, one launch (start us, length us, event | category | flops | bytes accessed | tf_op | source)
XLA Modules:
  0.0 73.5 jit_solution(16214109598358218316)
XLA Ops:
  0.0 0.0 copy-start
  0.0 0.0 copy-start.3
  0.0 0.0 copy-start.1
  0.0 3.4 %fusion.1 = f32[1024,64]{0,1:T(8,128)S(1)} fusion(bf16[1024,1792]{1,0:T(8,128)(2,1)} %bitcast.18, bf16[64,1792]{1,0:T(8,128)(2,1)} %param.10), kind=kOutput, calls=%fused_computation.5 | convolution fusion | flops 234881024 | bytes 4161536 | tf_op jit(solution)/shard_map/dot_general | solution.py:197
  3.4 0.0 copy-start.4
  3.4 0.0 copy-done.3
  3.4 0.0 copy-done.1
  3.5 0.0 copy-start.2
  3.5 1.2 %fusion.3 = f32[1024,64]{0,1:T(8,128)S(1)} fusion(bf16[1024,1792]{1,0:T(8,128)(2,1)S(1)} %bitcast.19, bf16[64,1792]{1,0:T(8,128)(2,1)S(1)} %copy-done.3), kind=kOutput, calls=%fused_computation.7 | convolution fusion | flops 234881024 | bytes 4161536 | tf_op jit(solution)/shard_map/dot_general | solution.py:197
  4.7 0.0 copy-done
  4.7 0.0 copy-done.4
  4.7 0.4 fusion.2
  5.1 0.0 copy-done.2
  5.1 0.4 fusion.4
  5.6 0.1 fusion
  5.7 3.3 %collective-permute-start = (f32[1024,128]{0,1:T(8,128)S(1)}, f32[1024,128]{0,1:T(8,128)S(1)}, u32[]{:S(2)}, u32[]{:S(2)}) collective-permute-start(f32[1024,128]{0,1:T(8,128)S(1)} %fusion), channel_id=1, source_target_pairs={{0,1},{1,0},{2,3},{3,2},{4,5},{5,4},{6,7},{7,6},{8,9},{9,8},{10,11... | collective-permute-start | bytes 1572872 | tf_op jit(solution)/shard_map/ppermute | solution.py:217
  9.0 1.5 %collective-permute-done = f32[1024,128]{0,1:T(8,128)S(1)} collective-permute-done((f32[1024,128]{0,1:T(8,128)S(1)}, f32[1024,128]{0,1:T(8,128)S(1)}, u32[]{:S(2)}, u32[]{:S(2)}) %collective-permute-start) | collective-permute-done | bytes 524320 | tf_op jit(solution)/shard_map/ppermute | solution.py:217
  10.5 0.1 select_add_fusion
  10.6 1.0 %copy.7 = f32[1024,128]{1,0:T(8,128)} copy(f32[1024,128]{0,1:T(8,128)S(1)} %select_add_fusion) | data formatting | bytes 1048576 | tf_op jit(solution)/shard_map/add | solution.py:218
  11.6 3.5 %all-to-all-start = ((f32[4,256,128]{2,1,0:T(8,128)}), f32[4,256,128]{2,1,0:T(8,128)S(1)}, u32[]{:S(2)}, u32[]{:S(2)}) async-start(f32[4,256,128]{2,1,0:T(8,128)} %bitcast.8), calls=%async_computation | async-start | bytes 1048576 | tf_op jit(solution)/shard_map/all_to_all | solution.py:207
  15.1 0.1 pad_add_fusion.place
  15.2 9.1 %all-to-all-done.parts = f32[4,256,128]{2,1,0:T(8,128)S(1)} async-done(((f32[4,256,128]{2,1,0:T(8,128)}), f32[4,256,128]{2,1,0:T(8,128)S(1)}, u32[]{:S(2)}, u32[]{:S(2)}) %all-to-all-start) | async-done | bytes 524320 | tf_op jit(solution)/shard_map/all_to_all | solution.py:207
  24.3 1.0 %shard_map.64 = (f32[8,40,128]{2,1,0:T(8,128)S(1)}, f32[32,128]{1,0:T(8,128)S(1)}) custom-call(s32[4]{0:T(128)S(1)} %pad_add_fusion.place, f32[4,256,128]{2,1,0:T(8,128)S(1)} %all-to-all-done.parts), custom_call_target="tpu_custom_call" | custom-call | tf_op jit(solution)/shard_map/pallas_call | solution.py:24
  25.3 15.0 %all_to_all.20.got = f32[8,40,128]{2,1,0:T(8,128)S(1)} all-to-all(f32[8,40,128]{2,1,0:T(8,128)S(1)} %get-tuple-element.7), channel_id=1, replica_groups=mesh['x'=4,'z'=8,'y'=4,'c'=2] {'z'}, dimensions={0} | all-to-all | bytes 327680 | tf_op jit(solution)/shard_map/all_to_all | solution.py:207
  40.3 0.6 shard_map.65
  40.9 13.9 %all_to_all.21.got = f32[16,72,128]{2,1,0:T(8,128)S(1)} all-to-all(f32[16,72,128]{2,1,0:T(8,128)S(1)} %shard_map.65), channel_id=1, replica_groups=mesh['x'=4,'z'=8,'y'=4,'c'=2] {'x','y'}, dimensions={0} | all-to-all | bytes 1179648 | tf_op jit(solution)/shard_map/all_to_all | solution.py:207
  54.8 3.3 %shard_map.66 = f32[32,128]{1,0:T(8,128)S(1)} custom-call(s32[4]{0:T(128)S(1)} %pad_add_fusion.place, f32[16,72,128]{2,1,0:T(8,128)S(1)} %all_to_all.21.got), custom_call_target="tpu_custom_call" | custom-call | tf_op jit(solution)/shard_map/pallas_call | solution.py:24
  58.1 4.4 %collective-permute-start.1 = (f32[32,128]{1,0:T(8,128)S(1)}, f32[32,128]{1,0:T(8,128)S(1)}, u32[]{:S(2)}, u32[]{:S(2)}) collective-permute-start(f32[32,128]{1,0:T(8,128)S(1)} %shard_map.66), channel_id=1, source_target_pairs={{0,1},{1,0},{2,3},{3,2},{4,5},{5,4},{6,7},{7,6},{8,9},{9,8},{10,11... | collective-permute-start | bytes 49160 | tf_op jit(solution)/shard_map/ppermute | solution.py:229
  62.4 0.8 %collective-permute-done.1.ready = f32[32,128]{1,0:T(8,128)S(1)} collective-permute-done((f32[32,128]{1,0:T(8,128)S(1)}, f32[32,128]{1,0:T(8,128)S(1)}, u32[]{:S(2)}, u32[]{:S(2)}) %collective-permute-start.1) | collective-permute-done | bytes 16416 | tf_op jit(solution)/shard_map/ppermute | solution.py:229
  63.3 1.5 %shard_map.67 = f32[8,8,128]{2,1,0:T(8,128)S(1)} custom-call(s32[4]{0:T(128)S(1)} %pad_add_fusion.place, f32[16,72,128]{2,1,0:T(8,128)S(1)} %all_to_all.21.got, f32[32,128]{1,0:T(8,128)S(1)} %collective-permute-done.1.ready), custom_call_target="tpu_custom_call" | custom-call | tf_op jit(solution)/shard_map/pallas_call | solution.py:24
  64.8 7.5 %all_to_all.22.got = f32[8,8,128]{2,1,0:T(8,128)S(1)} all-to-all(f32[8,8,128]{2,1,0:T(8,128)S(1)} %shard_map.67), channel_id=1, replica_groups=mesh['x'=4,'z'=8,'y'=4,'c'=2] {'y','c'}, dimensions={0} | all-to-all | bytes 65536 | tf_op jit(solution)/shard_map/all_to_all | solution.py:207
  72.3 1.1 %shard_map.68 = f32[4,128]{1,0:T(4,128)} custom-call(s32[4]{0:T(128)S(1)} %pad_add_fusion.place, f32[8,8,128]{2,1,0:T(8,128)S(1)} %all_to_all.22.got), custom_call_target="tpu_custom_call" | custom-call | tf_op jit(solution)/shard_map/pallas_call | solution.py:24
Async XLA Ops:
  0.0 4.7 %copy-start = (bf16[4,256,512]{2,1,0:T(8,128)(2,1)S(1)}, bf16[4,256,512]{2,1,0:T(8,128)(2,1)}, u32[]{:S(2)}) copy-start(bf16[4,256,512]{2,1,0:T(8,128)(2,1)} %param.7) | copy-start | bytes 3145732
  0.0 3.4 %copy-start.3 = (bf16[64,1792]{1,0:T(8,128)(2,1)S(1)}, bf16[64,1792]{1,0:T(8,128)(2,1)}, u32[]{:S(2)}) copy-start(bf16[64,1792]{1,0:T(8,128)(2,1)} %param.10) | copy-start | bytes 688132
  0.0 3.4 %copy-start.1 = (bf16[4,256,1792]{2,1,0:T(8,128)(2,1)S(1)}, bf16[4,256,1792]{2,1,0:T(8,128)(2,1)}, u32[]{:S(2)}) copy-start(bf16[4,256,1792]{2,1,0:T(8,128)(2,1)} %param.8) | copy-start | bytes 11010052
  3.4 1.3 %copy-start.4 = (bf16[64,512]{1,0:T(8,128)(2,1)S(1)}, bf16[64,512]{1,0:T(8,128)(2,1)}, u32[]{:S(2)}) copy-start(bf16[64,512]{1,0:T(8,128)(2,1)} %param.11) | copy-start | bytes 196612
  3.5 1.7 %copy-start.2 = (bf16[4,256,512]{2,1,0:T(8,128)(2,1)S(1)}, bf16[4,256,512]{2,1,0:T(8,128)(2,1)}, u32[]{:S(2)}) copy-start(bf16[4,256,512]{2,1,0:T(8,128)(2,1)} %param.9) | copy-start | bytes 3145732
  5.7 4.9 %collective-permute-start = (f32[1024,128]{0,1:T(8,128)S(1)}, f32[1024,128]{0,1:T(8,128)S(1)}, u32[]{:S(2)}, u32[]{:S(2)}) collective-permute-start(f32[1024,128]{0,1:T(8,128)S(1)} %fusion), channel_id=1, source_target_pairs={{0,1},{1,0},{2,3},{3,2},{4,5},{5,4},{6,7},{7,6},{8,9},{9,8},{10,11... | collective-permute-start | bytes 1572872 | tf_op jit(solution)/shard_map/ppermute | solution.py:217
  11.6 12.7 %all-to-all-start = ((f32[4,256,128]{2,1,0:T(8,128)}), f32[4,256,128]{2,1,0:T(8,128)S(1)}, u32[]{:S(2)}, u32[]{:S(2)}) async-start(f32[4,256,128]{2,1,0:T(8,128)} %bitcast.8), calls=%async_computation | async-start | bytes 1048576 | tf_op jit(solution)/shard_map/all_to_all | solution.py:207
  58.1 5.2 %collective-permute-start.1 = (f32[32,128]{1,0:T(8,128)S(1)}, f32[32,128]{1,0:T(8,128)S(1)}, u32[]{:S(2)}, u32[]{:S(2)}) collective-permute-start(f32[32,128]{1,0:T(8,128)S(1)} %shard_map.66), channel_id=1, source_target_pairs={{0,1},{1,0},{2,3},{3,2},{4,5},{5,4},{6,7},{7,6},{8,9},{9,8},{10,11... | collective-permute-start | bytes 49160 | tf_op jit(solution)/shard_map/ppermute | solution.py:229

commit v2 on v1

--- a/solution.py
+++ b/solution.py
@@ -11,7 +11,6 @@
 damping = 0.1
 RANK = 64
 LANES = 128
-PANEL = 8
 HIGH = lax.Precision.HIGHEST
 
 VM = pl.BlockSpec(memory_space=pltpu.VMEM)
@@ -50,11 +49,19 @@
     return jnp.concatenate([packed, pltpu.roll(packed, RANK, 1)], axis=0)
 
 
+def split(value):
+    high = value.astype(jnp.bfloat16)
+    return high, (value - high.astype(jnp.float32)).astype(jnp.bfloat16)
+
+
 def gram_kernel(place, parts, send, own):
     total = (parts[0] + parts[1]) + (parts[2] + parts[3])
-    gram = lax.dot_general(
-        total, total, (((0,), (0,)), ((), ())), precision=HIGH, preferred_element_type=jnp.float32
-    )
+    terms = jnp.concatenate(split(total), axis=0)
+    grams = lax.dot_general(
+        terms, terms, (((1,), (1,)), ((), ())), preferred_element_type=jnp.float32
+    )
+    high, low = grams[:LANES], grams[LANES:]
+    gram = high[:, :LANES] + ((high[:, LANES:] + low[:, :LANES]) + low[:, LANES:])
     top = gram[:RANK]
     low = gram[RANK:]
     side_out = pltpu.roll(low, RANK, 1)
@@ -96,30 +103,49 @@
 
 def invert(wide):
     lane = iota((1, LANES), 1)
-    sub = iota((RANK, 1), 0)
+    sub = iota((8, 1), 0)
     left = lane < RANK
     inner = lane & (RANK - 1)
-    for start in range(0, RANK, PANEL):
-        columns = [
-            jnp.where(
-                left,
-                jnp.broadcast_to(wide[:, k : k + 1], (RANK, LANES)),
-                jnp.broadcast_to(wide[:, RANK + k : RANK + k + 1], (RANK, LANES)),
-            )
-            for k in range(start, start + PANEL)
-        ]
-        for step in range(PANEL):
-            k = start + step
-            column = columns[step]
-            inverse = 1.0 / column[k : k + 1]
-            here = inner == k
-            scaled = jnp.where(here, inverse, wide[k : k + 1] * inverse)
-            is_row = sub == k
-            wide = jnp.where(is_row, scaled, jnp.where(here, 0.0, wide) - column * scaled)
-            for later in range(step + 1, PANEL):
-                ratio = columns[later][k : k + 1] * inverse
-                columns[later] = jnp.where(is_row, ratio, columns[later] - column * ratio)
-    return wide
+    blocks = [wide[8 * i : 8 * i + 8] for i in range(RANK // 8)]
+
+    def spread(block, k):
+        index = jnp.broadcast_to(jnp.where(left, k, RANK + k), (8, LANES))
+        return jnp.take_along_axis(block, index, axis=1, mode="promise_in_bounds")
+
+    def row_of(block, k):
+        return jnp.broadcast_to(block[k : k + 1], (8, LANES))
+
+    for at in range(RANK // 8):
+        columns = [[spread(block, k) for block in blocks] for k in range(8 * at, 8 * at + 8)]
+        for first in range(0, 8, 2):
+            second = first + 1
+            one, two = columns[first], columns[second]
+            a, b = row_of(one[at], first), row_of(two[at], first)
+            c, d = row_of(one[at], second), row_of(two[at], second)
+            inverse = 1.0 / (a * d - b * c)
+
+            def solve(upper, lower):
+                return (d * upper - b * lower) * inverse, (a * lower - c * upper) * inverse
+
+            is_first, is_second = sub == first, sub == second
+            for later in range(second + 1, 8):
+                column = columns[later]
+                up, down = solve(row_of(column[at], first), row_of(column[at], second))
+                column = [x - y * up - z * down for x, y, z in zip(column, one, two)]
+                column[at] = jnp.where(is_first, up, jnp.where(is_second, down, column[at]))
+                columns[later] = column
+            here = inner == 8 * at + first
+            there = inner == 8 * at + second
+            rows = blocks[at]
+            up, down = solve(row_of(rows, first), row_of(rows, second))
+            up = jnp.where(here, d * inverse, jnp.where(there, -b * inverse, up))
+            down = jnp.where(here, -c * inverse, jnp.where(there, a * inverse, down))
+            both = here | there
+            blocks = [
+                jnp.where(both, 0.0, x) - y * up - z * down for x, y, z in zip(blocks, one, two)
+            ]
+            blocks[at] = jnp.where(is_first, up, jnp.where(is_second, down, blocks[at]))
+    return jnp.concatenate(blocks, axis=0)
 
 
 def ready_kernel(total_tokens, place, got, out, held):
@@ -141,17 +167,19 @@
     held[...] = pltpu.roll(wide, RANK, 1)
     inverse_in = wide[:, :RANK]
     share = pl.multiple_of(place[2] * 8, 8)
-    inverse_out = jnp.concatenate(
-        [held[pl.ds(share, 8), :RANK], held[pl.ds(share + 32, 8), :RANK]], axis=0
-    )
+    inverse_out = jnp.concatenate([held[pl.ds(share, 8)], held[pl.ds(share + 32, 8)]], axis=0)
+    halves = jnp.concatenate([inverse_out[:, :32], inverse_out[:, 32:RANK]], axis=0)
+    grads = jnp.concatenate([got[place[0] * 4 + seq, 40:72] for seq in range(4)], axis=1)
+    products = jnp.dot(halves, grads, precision=HIGH, preferred_element_type=jnp.float32)
     lefts = []
     for seq in range(4):
-        grad = unpack(got[place[0] * 4 + seq, 40:72])[:, :RANK]
-        lefts.append(
-            jnp.dot(inverse_out, grad, precision=HIGH, preferred_element_type=jnp.float32)
-        )
+        product = products[:, LANES * seq : LANES * seq + LANES]
+        lefts.append(product[:16] + pltpu.roll(product[16:], RANK, 1))
     ready = jnp.dot(
-        jnp.concatenate(lefts, axis=0), inverse_in, precision=HIGH, preferred_element_type=jnp.float32
+        jnp.concatenate(lefts, axis=0)[:, :RANK],
+        inverse_in,
+        precision=HIGH,
+        preferred_element_type=jnp.float32,
     )
     ready = jnp.concatenate([ready, ready], axis=1)
     half = iota((8, LANES), 1) < RANK
@@ -168,13 +196,12 @@
             for y in range(4):
                 tiles.append(got[x * 4 + y, 8 * z : 8 * z + 8])
     queries = jnp.concatenate(tiles, axis=0)
-    pairs = lax.dot_general(
-        queries,
-        ready[...],
-        (((1,), (1,)), ((), ())),
-        precision=HIGH,
-        preferred_element_type=jnp.float32,
-    )
+    high, low = split(queries)
+    both = jnp.concatenate(split(ready[...]), axis=0)
+    dims = (((1,), (1,)), ((), ()))
+    pairs = lax.dot_general(high, both, dims, preferred_element_type=jnp.float32)
+    pairs += lax.dot_general(low, both, dims, preferred_element_type=jnp.float32)
+    pairs = pairs[:, :32] + pairs[:, 32:]
     count = len(tiles)
     same = (iota((8 * count, 32), 0) & 7) == (iota((8 * count, 32), 1) & 7)
     sums = jnp.where(same, pairs, 0.0).reshape(count, 8, 32).sum(axis=1)
@@ -186,21 +213,11 @@
         send[peer] = scores
 
 
-def total_kernel(place, got, out):
-    total = (got[1] + got[3]) + (got[5] + got[7])
-    out[...] = total[:4]
-
-
 def features(acts, grads, proj_in, proj_out):
-    rows_in = acts.reshape(-1, acts.shape[-1])
-    rows_out = grads.reshape(-1, grads.shape[-1])
-    feat_in = lax.dot_general(
-        rows_in, proj_in, (((1,), (1,)), ((), ())), preferred_element_type=jnp.float32
-    )
-    feat_out = lax.dot_general(
-        rows_out, proj_out, (((1,), (1,)), ((), ())), preferred_element_type=jnp.float32
-    )
-    return jnp.concatenate([feat_in, feat_out], axis=1)
+    dims = (((1,), (2,)), ((), ()))
+    feat_in = lax.dot_general(proj_in, acts, dims, preferred_element_type=jnp.float32)
+    feat_out = lax.dot_general(proj_out, grads, dims, preferred_element_type=jnp.float32)
+    return jnp.concatenate([feat_in, feat_out], axis=0).transpose(1, 0, 2)
 
 
 def swap(value, axis):
@@ -216,20 +233,22 @@
     query = features(query_acts, query_grads, proj_in, proj_out)
     other = lax.ppermute(jnp.where(is_train, query, train), "c", [(0, 1), (1, 0)])
     mine = jnp.where(is_train, train, query) + other
-    parts = swap(mine.reshape(4, seq_len, LANES), "y")
+    place, mine = lax.optimization_barrier((place, mine))
+    parts = swap(mine, "y")
     send, own = call(gram_kernel, (f32(8, 40, LANES), f32(32, LANES)))(place, parts)
     got = swap(send, "z")
     send = call(spread_kernel, f32(16, 72, LANES))(place, got, own)
     got = swap(send, ("x", "y"))
+    queries = lax.ppermute(got, "c", [(0, 1), (1, 0)])
     ready = call(
         functools.partial(ready_kernel, total_tokens),
         f32(32, LANES),
         [pltpu.VMEM((RANK, LANES), jnp.float32)],
     )(place, got)
-    ready = lax.ppermute(ready, "c", [(0, 1), (1, 0)])
     scale = 1.0 / (seq_len * RANK)
-    send = call(functools.partial(score_kernel, scale), f32(8, 8, LANES))(place, got, ready)
-    return call(total_kernel, f32(4, LANES))(place, swap(send, ("y", "c")))
+    send = call(functools.partial(score_kernel, scale), f32(8, 8, LANES))(place, queries, ready)
+    got = swap(send, ("y", "c"))
+    return ((got[0] + got[2]) + (got[4] + got[6]))[:4]
 
 
 def solution(mesh):

time: 73.7 us -> 70.2 us (0.953)
  blocking collectives: 36.5 us -> 48.4 us
  waiting for transfers between devices: 11.5 us -> 1.46 us
  starting transfers between devices: 11.2 us -> 7.86 us
  Pallas kernels: 7.48 us -> 5.63 us
    all_to_all x3 -> x4, blocking collectives: 36.5 us -> 48.4 us  [swap(): return lax.all_to_all(value, axis, 0, 0, tiled=True)]
    all_to_all x1 -> x0, waiting for transfers between devices: 9.11 us -> none  [swap(): return lax.all_to_all(value, axis, 0, 0, tiled=True)]
    all_to_all x1 -> x0, starting transfers between devices: 3.47 us -> none  [swap(): return lax.all_to_all(value, axis, 0, 0, tiled=True)]
    pallas_call x5 -> x4, Pallas kernels: 7.48 us -> 5.63 us  [wrapped(): pl.pallas_call(body, out_shape=out, in_specs=[SM] + [VM] * (len(args) - 1...]
    add x1 -> x0, local copies, waits for them, and re-layouts: 1 us -> none  [on_device(): mine = jnp.where(is_train, train, query) + other]
    ppermute x1, waiting for transfers between devices: 0.84 us -> 0.01 us  [on_device(): queries = lax.ppermute(got, 'c', [(0, 1), (1, 0)])]
  transfers between devices with their start and end apart: 3 -> 2, of which waited for: 3 -> 1; matrix products, arithmetic and copies ran while one was open for 0% -> 0% of each run, Pallas kernels for 0% -> 4%
where the time goes in v2:
time: 70.2 us; the launch traced here: 70 us
  blocking collectives  48.4 us (69%)
  starting transfers between devices  7.86 us (11%)
  Pallas kernels  5.63 us (8%)
  matrix products  5.58 us (8%)
  waiting for transfers between devices  1.46 us (2%)
    all_to_all x4, blocking collectives, swap(): return lax.all_to_all(value, axis, 0, 0, tiled=True)  48.4 us
    pallas_call x4, Pallas kernels, wrapped(): pl.pallas_call(body, out_shape=out, in_specs=[SM] + [VM] * (len(args) - 1...  5.63 us
    dot_general x2, matrix products, features(): lax.dot_general(proj_in, acts, dims, preferred_element_type=jnp.float32)  4.72 us
    ppermute x1, starting transfers between devices, on_device(): queries = lax.ppermute(got, 'c', [(0, 1), (1, 0)])  4.55 us
    ppermute x1, starting transfers between devices, on_device(): lax.ppermute(jnp.where(is_train, query, train), 'c', [(0, 1), (1, 0)])  3.32 us
    ppermute x1, waiting for transfers between devices, on_device(): lax.ppermute(jnp.where(is_train, query, train), 'c', [(0, 1), (1, 0)])  1.46 us
  transfers between devices with their start and end apart: 2, of which 1 were waited for; matrix products, arithmetic and copies ran while one was open for 0% of the time, Pallas kernels for 4%

profile of v2, /device:TPU:1, one launch (start us, length us, event | category | flops | bytes accessed | tf_op | source)
XLA Modules:
  0.0 70.0 jit_solution(5712943162669941952)
XLA Ops:
  0.0 0.0 copy-start
  0.0 0.0 copy-start.3
  0.0 0.0 copy-start.1
  0.0 0.0 copy-start.4
  0.0 3.5 %fusion.2 = f32[64,4,256]{2,0,1:T(8,128)S(1)} fusion(bf16[4,256,1792]{2,1,0:T(8,128)(2,1)} %param.6, bf16[64,1792]{1,0:T(8,128)(2,1)} %param.10), kind=kOutput, calls=%fused_computation.6 | convolution fusion | flops 234881024 | bytes 4161536 | tf_op jit(solution)/shard_map/dot_general | solution.py:218
  3.5 0.0 copy-done.3
  3.5 0.0 copy-done.1
  3.6 0.0 copy-start.2
  3.6 1.2 %fusion = f32[64,4,256]{2,0,1:T(8,128)S(1)} fusion(bf16[4,256,1792]{2,1,0:T(8,128)(2,1)S(1)} %copy-done.1, bf16[64,1792]{1,0:T(8,128)(2,1)S(1)} %copy-done.3), kind=kOutput, calls=%fused_computation.4 | convolution fusion | flops 234881024 | bytes 4161536 | tf_op jit(solution)/shard_map/dot_general | solution.py:218
  4.8 0.0 copy-done
  4.8 0.0 copy-done.4
  4.8 0.4 fusion.6
  5.2 0.0 copy-done.2
  5.2 0.4 fusion.4
  5.7 0.1 select_bitcast_fusion
  5.8 3.3 %collective-permute-start = (f32[4,128,256]{2,1,0:T(8,128)S(1)}, f32[4,128,256]{2,1,0:T(8,128)S(1)}, u32[]{:S(2)}, u32[]{:S(2)}) collective-permute-start(f32[4,128,256]{2,1,0:T(8,128)S(1)} %select_bitcast_fusion), channel_id=1, source_target_pairs={{0,1},{1,0},{2,3},{3,2},{4,5},{5,4},{6,7},{7,6},{8,9},{9,8},{10,11... | collective-permute-start | bytes 1572872 | tf_op jit(solution)/shard_map/ppermute | solution.py:234
  9.1 0.1 pad_add_fusion.place
  9.2 1.5 %collective-permute-done = f32[4,128,256]{2,1,0:T(8,128)S(1)} collective-permute-done((f32[4,128,256]{2,1,0:T(8,128)S(1)}, f32[4,128,256]{2,1,0:T(8,128)S(1)}, u32[]{:S(2)}, u32[]{:S(2)}) %collective-permute-start) | collective-permute-done | bytes 524320 | tf_op jit(solution)/shard_map/ppermute | solution.py:234
  10.6 0.1 bitcast_add_fusion
  10.7 11.5 %all_to_all.20.parts = f32[4,128,256]{2,1,0:T(8,128)S(1)} all-to-all(f32[4,128,256]{2,1,0:T(8,128)S(1)} %bitcast_add_fusion), channel_id=1, replica_groups=mesh['x'=4,'z'=8,'y'=4,'c'=2] {'y'}, dimensions={0} | all-to-all | bytes 1048576 | tf_op jit(solution)/shard_map/all_to_all | solution.py:224
  22.2 0.9 %shard_map.64 = (f32[8,40,128]{2,1,0:T(8,128)S(1)}, f32[32,128]{1,0:T(8,128)S(1)}) custom-call(s32[4]{0:T(128)S(1)} %pad_add_fusion.place, f32[4,128,256]{2,1,0:T(8,128)S(1)} %all_to_all.20.parts), custom_call_target="tpu_custom_call" | custom-call | tf_op jit(solution)/shard_map/pallas_call | solution.py:23
  23.1 15.8 %all_to_all.21.got = f32[8,40,128]{2,1,0:T(8,128)S(1)} all-to-all(f32[8,40,128]{2,1,0:T(8,128)S(1)} %get-tuple-element.11), channel_id=1, replica_groups=mesh['x'=4,'z'=8,'y'=4,'c'=2] {'z'}, dimensions={0} | all-to-all | bytes 327680 | tf_op jit(solution)/shard_map/all_to_all | solution.py:224
  38.9 0.6 shard_map.65
  39.5 13.9 %all_to_all.22.got = f32[16,72,128]{2,1,0:T(8,128)S(1)} all-to-all(f32[16,72,128]{2,1,0:T(8,128)S(1)} %shard_map.65), channel_id=1, replica_groups=mesh['x'=4,'z'=8,'y'=4,'c'=2] {'x','y'}, dimensions={0} | all-to-all | bytes 1179648 | tf_op jit(solution)/shard_map/all_to_all | solution.py:224
  53.4 4.5 %collective-permute-start.1 = (f32[16,72,128]{2,1,0:T(8,128)S(1)}, f32[16,72,128]{2,1,0:T(8,128)S(1)}, u32[]{:S(2)}, u32[]{:S(2)}) collective-permute-start(f32[16,72,128]{2,1,0:T(8,128)S(1)} %all_to_all.22.got), channel_id=1, source_target_pairs={{0,1},{1,0},{2,3},{3,2},{4,5},{5,4},{6,7},{7,6},{8,9},{9,8},{10,11... | collective-permute-start | bytes 1769480 | tf_op jit(solution)/shard_map/ppermute | solution.py:242
  57.9 2.8 %shard_map.66.ready = f32[32,128]{1,0:T(8,128)S(1)} custom-call(s32[4]{0:T(128)S(1)} %pad_add_fusion.place, f32[16,72,128]{2,1,0:T(8,128)S(1)} %all_to_all.22.got), custom_call_target="tpu_custom_call" | custom-call | tf_op jit(solution)/shard_map/pallas_call | solution.py:23
  60.7 0.0 collective-permute-done.1.got
  60.7 1.3 %shard_map.67 = f32[8,8,128]{2,1,0:T(8,128)S(1)} custom-call(s32[4]{0:T(128)S(1)} %pad_add_fusion.place, f32[16,72,128]{2,1,0:T(8,128)S(1)} %collective-permute-done.1.got, f32[32,128]{1,0:T(8,128)S(1)} %shard_map.66.ready), custom_call_target="tpu_custom_call" | custom-call | tf_op jit(solution)/shard_map/pallas_call | solution.py:23
  62.1 7.3 %all_to_all.23 = f32[8,8,128]{2,1,0:T(8,128)S(1)} all-to-all(f32[8,8,128]{2,1,0:T(8,128)S(1)} %shard_map.67), channel_id=1, replica_groups=mesh['x'=4,'z'=8,'y'=4,'c'=2] {'y','c'}, dimensions={0} | all-to-all | bytes 65536 | tf_op jit(solution)/shard_map/all_to_all | solution.py:224
  69.4 0.6 slice_bitcast_fusion
  (1 shorter events, 0.0 us)
Async XLA Ops:
  0.0 4.8 %copy-start = (bf16[4,256,512]{2,1,0:T(8,128)(2,1)S(1)}, bf16[4,256,512]{2,1,0:T(8,128)(2,1)}, u32[]{:S(2)}) copy-start(bf16[4,256,512]{2,1,0:T(8,128)(2,1)} %param.7) | copy-start | bytes 3145732
  0.0 3.5 %copy-start.3 = (bf16[64,1792]{1,0:T(8,128)(2,1)S(1)}, bf16[64,1792]{1,0:T(8,128)(2,1)}, u32[]{:S(2)}) copy-start(bf16[64,1792]{1,0:T(8,128)(2,1)} %param.10) | copy-start | bytes 688132
  0.0 3.5 %copy-start.1 = (bf16[4,256,1792]{2,1,0:T(8,128)(2,1)S(1)}, bf16[4,256,1792]{2,1,0:T(8,128)(2,1)}, u32[]{:S(2)}) copy-start(bf16[4,256,1792]{2,1,0:T(8,128)(2,1)} %param.8) | copy-start | bytes 11010052
  0.0 4.8 %copy-start.4 = (bf16[64,512]{1,0:T(8,128)(2,1)S(1)}, bf16[64,512]{1,0:T(8,128)(2,1)}, u32[]{:S(2)}) copy-start(bf16[64,512]{1,0:T(8,128)(2,1)} %param.11) | copy-start | bytes 196612
  3.6 1.7 %copy-start.2 = (bf16[4,256,512]{2,1,0:T(8,128)(2,1)S(1)}, bf16[4,256,512]{2,1,0:T(8,128)(2,1)}, u32[]{:S(2)}) copy-start(bf16[4,256,512]{2,1,0:T(8,128)(2,1)} %param.9) | copy-start | bytes 3145732
  5.8 4.9 %collective-permute-start = (f32[4,128,256]{2,1,0:T(8,128)S(1)}, f32[4,128,256]{2,1,0:T(8,128)S(1)}, u32[]{:S(2)}, u32[]{:S(2)}) collective-permute-start(f32[4,128,256]{2,1,0:T(8,128)S(1)} %select_bitcast_fusion), channel_id=1, source_target_pairs={{0,1},{1,0},{2,3},{3,2},{4,5},{5,4},{6,7},{7,6},{8,9},{9,8},{10,11... | collective-permute-start | bytes 1572872 | tf_op jit(solution)/shard_map/ppermute | solution.py:234
  53.4 7.4 %collective-permute-start.1 = (f32[16,72,128]{2,1,0:T(8,128)S(1)}, f32[16,72,128]{2,1,0:T(8,128)S(1)}, u32[]{:S(2)}, u32[]{:S(2)}) collective-permute-start(f32[16,72,128]{2,1,0:T(8,128)S(1)} %all_to_all.22.got), channel_id=1, source_target_pairs={{0,1},{1,0},{2,3},{3,2},{4,5},{5,4},{6,7},{7,6},{8,9},{9,8},{10,11... | collective-permute-start | bytes 1769480 | tf_op jit(solution)/shard_map/ppermute | solution.py:242

commit v3 on v2

--- a/solution.py
+++ b/solution.py
@@ -9,12 +9,12 @@
 from jax.sharding import PartitionSpec as P
 
 damping = 0.1
+TRAIN_CORE = 1
 RANK = 64
 LANES = 128
 HIGH = lax.Precision.HIGHEST
 
 VM = pl.BlockSpec(memory_space=pltpu.VMEM)
-SM = pl.BlockSpec(memory_space=pltpu.SMEM)
 PARAMS = pltpu.CompilerParams(vmem_limit_bytes=32 * 1024 * 1024)
 
 
@@ -23,7 +23,7 @@
         return pl.pallas_call(
             body,
             out_shape=out,
-            in_specs=[SM] + [VM] * (len(args) - 1),
+            in_specs=[VM] * len(args),
             out_specs=jax.tree.map(lambda _: VM, out),
             scratch_shapes=list(scratch),
             compiler_params=PARAMS,
@@ -54,7 +54,7 @@
     return high, (value - high.astype(jnp.float32)).astype(jnp.bfloat16)
 
 
-def gram_kernel(place, parts, send, own):
+def gram_kernel(parts, send, own):
     total = (parts[0] + parts[1]) + (parts[2] + parts[3])
     terms = jnp.concatenate(split(total), axis=0)
     grams = lax.dot_general(
@@ -71,7 +71,7 @@
     diag = jnp.sum(jnp.where(row == lane, side_out, 0.0), axis=0, keepdims=True)
     grad = pack(low)
     own[...] = grad
-    is_train = place[3] == 0
+    is_train = lax.axis_index("c") == TRAIN_CORE
     first = jnp.where(is_train, both, grad)
     rest = jnp.broadcast_to(diag, (8, LANES))
     for peer in range(send.shape[0]):
@@ -79,8 +79,8 @@
         send[peer, 32:40] = rest
 
 
-def spread_kernel(place, got, own, send):
-    @pl.when(place[3] == 0)
+def spread_kernel(got, own, send):
+    @pl.when(lax.axis_index("c") == TRAIN_CORE)
     def _():
         total = got[0]
         for peer in range(1, got.shape[0]):
@@ -90,7 +90,7 @@
             send[peer, :40] = total
             send[peer, 40:72] = grad
 
-    @pl.when(place[3] != 0)
+    @pl.when(lax.axis_index("c") != TRAIN_CORE)
     def _():
         for share in range(4):
             for query in range(got.shape[0]):
@@ -148,48 +148,54 @@
     return jnp.concatenate(blocks, axis=0)
 
 
-def ready_kernel(total_tokens, place, got, out, held):
-    total = got[0, :40]
-    for peer in range(1, got.shape[0]):
-        total = total + got[peer, :40]
-    both = unpack(total[:32])[:, :RANK]
-    flipped = both.T
-    diag = total[32:33, :RANK]
-    row = iota((RANK, RANK), 0)
-    lane = iota((RANK, RANK), 1)
-    factor_in = jnp.where(row <= lane, both, flipped)
-    factor_out = jnp.where(row > lane, both, jnp.where(row == lane, diag, flipped))
-    eye = jnp.where(row == lane, damping, 0.0)
-    wide = jnp.concatenate(
-        [factor_in * (1.0 / total_tokens) + eye, factor_out * (1.0 / total_tokens) + eye], axis=1
-    )
-    wide = invert(wide)
-    held[...] = pltpu.roll(wide, RANK, 1)
-    inverse_in = wide[:, :RANK]
-    share = pl.multiple_of(place[2] * 8, 8)
-    inverse_out = jnp.concatenate([held[pl.ds(share, 8)], held[pl.ds(share + 32, 8)]], axis=0)
-    halves = jnp.concatenate([inverse_out[:, :32], inverse_out[:, 32:RANK]], axis=0)
-    grads = jnp.concatenate([got[place[0] * 4 + seq, 40:72] for seq in range(4)], axis=1)
-    products = jnp.dot(halves, grads, precision=HIGH, preferred_element_type=jnp.float32)
-    lefts = []
-    for seq in range(4):
-        product = products[:, LANES * seq : LANES * seq + LANES]
-        lefts.append(product[:16] + pltpu.roll(product[16:], RANK, 1))
-    ready = jnp.dot(
-        jnp.concatenate(lefts, axis=0)[:, :RANK],
-        inverse_in,
-        precision=HIGH,
-        preferred_element_type=jnp.float32,
-    )
-    ready = jnp.concatenate([ready, ready], axis=1)
-    half = iota((8, LANES), 1) < RANK
-    for seq in range(4):
-        out[8 * seq : 8 * seq + 8] = jnp.where(
-            half, ready[16 * seq : 16 * seq + 8], ready[16 * seq + 8 : 16 * seq + 16]
+def ready_kernel(total_tokens, got, out, held):
+    @pl.when(lax.axis_index("c") == TRAIN_CORE)
+    def _():
+        total = got[0, :40]
+        for peer in range(1, got.shape[0]):
+            total = total + got[peer, :40]
+        both = unpack(total[:32])[:, :RANK]
+        flipped = both.T
+        diag = total[32:33, :RANK]
+        row = iota((RANK, RANK), 0)
+        lane = iota((RANK, RANK), 1)
+        factor_in = jnp.where(row <= lane, both, flipped)
+        factor_out = jnp.where(row > lane, both, jnp.where(row == lane, diag, flipped))
+        eye = jnp.where(row == lane, damping, 0.0)
+        wide = jnp.concatenate(
+            [factor_in * (1.0 / total_tokens) + eye, factor_out * (1.0 / total_tokens) + eye], axis=1
         )
-
-
-def score_kernel(scale, place, got, ready, send):
+        wide = invert(wide)
+        held[...] = pltpu.roll(wide, RANK, 1)
+        inverse_in = wide[:, :RANK]
+        share = pl.multiple_of(lax.axis_index("y") * 8, 8)
+        inverse_out = jnp.concatenate([held[pl.ds(share, 8)], held[pl.ds(share + 32, 8)]], axis=0)
+        halves = jnp.concatenate([inverse_out[:, :32], inverse_out[:, 32:RANK]], axis=0)
+        grads = jnp.concatenate([got[lax.axis_index("x") * 4 + seq, 40:72] for seq in range(4)], axis=1)
+        products = jnp.dot(halves, grads, precision=HIGH, preferred_element_type=jnp.float32)
+        lefts = []
+        for seq in range(4):
+            product = products[:, LANES * seq : LANES * seq + LANES]
+            lefts.append(product[:16] + pltpu.roll(product[16:], RANK, 1))
+        ready = jnp.dot(
+            jnp.concatenate(lefts, axis=0)[:, :RANK],
+            inverse_in,
+            precision=HIGH,
+            preferred_element_type=jnp.float32,
+        )
+        ready = jnp.concatenate([ready, ready], axis=1)
+        half = iota((8, LANES), 1) < RANK
+        for seq in range(4):
+            out[8 * seq : 8 * seq + 8] = jnp.where(
+                half, ready[16 * seq : 16 * seq + 8], ready[16 * seq + 8 : 16 * seq + 16]
+            )
+
+    @pl.when(lax.axis_index("c") != TRAIN_CORE)
+    def _():
+        out[...] = jnp.zeros_like(out)
+
+
+def score_kernel(scale, got, ready, send):
     tiles = []
     for x in range(4):
         for z in range(8):
@@ -227,26 +233,24 @@
 def on_device(train_acts, train_grads, query_acts, query_grads, proj_in, proj_out):
     seq_len = train_acts.shape[1]
     total_tokens = train_acts.shape[0] * seq_len * 32
-    place = jnp.stack([lax.axis_index(name) for name in ("x", "z", "y", "c")]).astype(jnp.int32)
-    is_train = place[3] == 0
+    is_train = lax.axis_index("c") == TRAIN_CORE
     train = features(train_acts, train_grads, proj_in, proj_out)
     query = features(query_acts, query_grads, proj_in, proj_out)
     other = lax.ppermute(jnp.where(is_train, query, train), "c", [(0, 1), (1, 0)])
     mine = jnp.where(is_train, train, query) + other
-    place, mine = lax.optimization_barrier((place, mine))
     parts = swap(mine, "y")
-    send, own = call(gram_kernel, (f32(8, 40, LANES), f32(32, LANES)))(place, parts)
+    send, own = call(gram_kernel, (f32(8, 40, LANES), f32(32, LANES)))(parts)
     got = swap(send, "z")
-    send = call(spread_kernel, f32(16, 72, LANES))(place, got, own)
+    send = call(spread_kernel, f32(16, 72, LANES))(got, own)
     got = swap(send, ("x", "y"))
-    queries = lax.ppermute(got, "c", [(0, 1), (1, 0)])
     ready = call(
         functools.partial(ready_kernel, total_tokens),
         f32(32, LANES),
         [pltpu.VMEM((RANK, LANES), jnp.float32)],
-    )(place, got)
+    )(got)
+    ready = lax.ppermute(ready, "c", [(0, 1), (1, 0)])
     scale = 1.0 / (seq_len * RANK)
-    send = call(functools.partial(score_kernel, scale), f32(8, 8, LANES))(place, queries, ready)
+    send = call(functools.partial(score_kernel, scale), f32(8, 8, LANES))(got, ready)
     got = swap(send, ("y", "c"))
     return ((got[0] + got[2]) + (got[4] + got[6]))[:4]
 

time: 70.2 us -> 66.8 us (0.952)
  starting transfers between devices: 7.86 us -> 5.55 us
  Pallas kernels: 5.63 us -> 3.48 us
  waiting for transfers between devices: 1.46 us -> 2.38 us
    ppermute x1, starting transfers between devices: 4.55 us -> 2.24 us  [on_device(): ready = lax.ppermute(ready, 'c', [(0, 1), (1, 0)])]
    pallas_call x4, Pallas kernels: 5.63 us -> 3.48 us  [wrapped(): pl.pallas_call(body, out_shape=out, in_specs=[VM] * len(args), out_specs=...]
    ppermute x1, waiting for transfers between devices: 0.01 us -> 0.84 us  [on_device(): ready = lax.ppermute(ready, 'c', [(0, 1), (1, 0)])]
  transfers between devices with their start and end apart: 2 -> 2, of which waited for: 1 -> 2; matrix products, arithmetic and copies ran while one was open for 0% -> 0% of each run, Pallas kernels for 4% -> 0%
where the time goes in v3:
time: 66.8 us; the launch traced here: 66.6 us
  blocking collectives  48.7 us (73%)
  matrix products  5.58 us (8%)
  starting transfers between devices  5.55 us (8%)
  Pallas kernels  3.48 us (5%)
  waiting for transfers between devices  2.38 us (4%)
    all_to_all x4, blocking collectives, swap(): return lax.all_to_all(value, axis, 0, 0, tiled=True)  48.7 us
    dot_general x2, matrix products, features(): lax.dot_general(proj_in, acts, dims, preferred_element_type=jnp.float32)  4.72 us
    pallas_call x4, Pallas kernels, wrapped(): pl.pallas_call(body, out_shape=out, in_specs=[VM] * len(args), out_specs=...  3.48 us
    ppermute x1, starting transfers between devices, on_device(): lax.ppermute(jnp.where(is_train, query, train), 'c', [(0, 1), (1, 0)])  3.32 us
    ppermute x1, starting transfers between devices, on_device(): ready = lax.ppermute(ready, 'c', [(0, 1), (1, 0)])  2.24 us
    ppermute x1, waiting for transfers between devices, on_device(): lax.ppermute(jnp.where(is_train, query, train), 'c', [(0, 1), (1, 0)])  1.54 us
  transfers between devices with their start and end apart: 2, of which 2 were waited for; matrix products, arithmetic and copies ran while one was open for 0% of the time, Pallas kernels for 0%

profile of v3, /device:TPU:1, one launch (start us, length us, event | category | flops | bytes accessed | tf_op | source)
XLA Modules:
  0.0 66.6 jit_solution(13579132825818782330)
XLA Ops:
  0.0 0.0 copy-start
  0.0 0.0 copy-start.3
  0.0 0.0 copy-start.1
  0.0 0.0 copy-start.4
  0.0 3.5 %fusion.2 = f32[64,4,256]{2,0,1:T(8,128)S(1)} fusion(bf16[4,256,1792]{2,1,0:T(8,128)(2,1)} %param.6, bf16[64,1792]{1,0:T(8,128)(2,1)} %param.10), kind=kOutput, calls=%fused_computation.6 | convolution fusion | flops 234881024 | bytes 4161536 | tf_op jit(solution)/shard_map/dot_general | solution.py:224
  3.5 0.0 copy-done.3
  3.5 0.0 copy-done.1
  3.6 0.0 copy-start.2
  3.6 1.2 %fusion = f32[64,4,256]{2,0,1:T(8,128)S(1)} fusion(bf16[4,256,1792]{2,1,0:T(8,128)(2,1)S(1)} %copy-done.1, bf16[64,1792]{1,0:T(8,128)(2,1)S(1)} %copy-done.3), kind=kOutput, calls=%fused_computation.4 | convolution fusion | flops 234881024 | bytes 4161536 | tf_op jit(solution)/shard_map/dot_general | solution.py:224
  4.8 0.0 copy-done
  4.8 0.0 copy-done.4
  4.8 0.4 fusion.6
  5.2 0.0 copy-done.2
  5.2 0.4 fusion.4
  5.7 0.1 select_bitcast_fusion
  5.8 3.3 %collective-permute-start = (f32[4,128,256]{2,1,0:T(8,128)S(1)}, f32[4,128,256]{2,1,0:T(8,128)S(1)}, u32[]{:S(2)}, u32[]{:S(2)}) collective-permute-start(f32[4,128,256]{2,1,0:T(8,128)S(1)} %select_bitcast_fusion), channel_id=1, source_target_pairs={{0,1},{1,0},{2,3},{3,2},{4,5},{5,4},{6,7},{7,6},{8,9},{9,8},{10,11... | collective-permute-start | bytes 1572872 | tf_op jit(solution)/shard_map/ppermute | solution.py:239
  9.1 1.5 %collective-permute-done = f32[4,128,256]{2,1,0:T(8,128)S(1)} collective-permute-done((f32[4,128,256]{2,1,0:T(8,128)S(1)}, f32[4,128,256]{2,1,0:T(8,128)S(1)}, u32[]{:S(2)}, u32[]{:S(2)}) %collective-permute-start) | collective-permute-done | bytes 524320 | tf_op jit(solution)/shard_map/ppermute | solution.py:239
  10.6 0.1 bitcast_add_fusion
  10.7 11.5 %all_to_all.20.parts = f32[4,128,256]{2,1,0:T(8,128)S(1)} all-to-all(f32[4,128,256]{2,1,0:T(8,128)S(1)} %bitcast_add_fusion), channel_id=1, replica_groups=mesh['x'=4,'z'=8,'y'=4,'c'=2] {'y'}, dimensions={0} | all-to-all | bytes 1048576 | tf_op jit(solution)/shard_map/all_to_all | solution.py:230
  22.2 0.4 shard_map.64
  22.6 15.8 %all_to_all.21.got = f32[8,40,128]{2,1,0:T(8,128)S(1)} all-to-all(f32[8,40,128]{2,1,0:T(8,128)S(1)} %get-tuple-element.7), channel_id=1, replica_groups=mesh['x'=4,'z'=8,'y'=4,'c'=2] {'z'}, dimensions={0} | all-to-all | bytes 327680 | tf_op jit(solution)/shard_map/all_to_all | solution.py:230
  38.4 13.9 %all_to_all.22.got = f32[16,72,128]{2,1,0:T(8,128)S(1)} all-to-all(f32[16,72,128]{2,1,0:T(8,128)S(1)} %shard_map.65), channel_id=1, replica_groups=mesh['x'=4,'z'=8,'y'=4,'c'=2] {'x','y'}, dimensions={0} | all-to-all | bytes 1179648 | tf_op jit(solution)/shard_map/all_to_all | solution.py:230
  52.3 2.3 %shard_map.66 = f32[32,128]{1,0:T(8,128)S(1)} custom-call(f32[16,72,128]{2,1,0:T(8,128)S(1)} %all_to_all.22.got), custom_call_target="tpu_custom_call" | custom-call | tf_op jit(solution)/shard_map/pallas_call | solution.py:23
  54.6 2.2 %collective-permute-start.1 = (f32[32,128]{1,0:T(8,128)S(1)}, f32[32,128]{1,0:T(8,128)S(1)}, u32[]{:S(2)}, u32[]{:S(2)}) collective-permute-start(f32[32,128]{1,0:T(8,128)S(1)} %shard_map.66), channel_id=1, source_target_pairs={{0,1},{1,0},{2,3},{3,2},{4,5},{5,4},{6,7},{7,6},{8,9},{9,8},{10,11... | collective-permute-start | bytes 49160 | tf_op jit(solution)/shard_map/ppermute | solution.py:251
  56.8 0.8 %collective-permute-done.1.ready = f32[32,128]{1,0:T(8,128)S(1)} collective-permute-done((f32[32,128]{1,0:T(8,128)S(1)}, f32[32,128]{1,0:T(8,128)S(1)}, u32[]{:S(2)}, u32[]{:S(2)}) %collective-permute-start.1) | collective-permute-done | bytes 16416 | tf_op jit(solution)/shard_map/ppermute | solution.py:251
  57.7 0.8 %shard_map.67 = f32[8,8,128]{2,1,0:T(8,128)S(1)} custom-call(f32[16,72,128]{2,1,0:T(8,128)S(1)} %all_to_all.22.got, f32[32,128]{1,0:T(8,128)S(1)} %collective-permute-done.1.ready), custom_call_target="tpu_custom_call" | custom-call | tf_op jit(solution)/shard_map/pallas_call | solution.py:23
  58.4 7.5 %all_to_all.23 = f32[8,8,128]{2,1,0:T(8,128)S(1)} all-to-all(f32[8,8,128]{2,1,0:T(8,128)S(1)} %shard_map.67), channel_id=1, replica_groups=mesh['x'=4,'z'=8,'y'=4,'c'=2] {'y','c'}, dimensions={0} | all-to-all | bytes 65536 | tf_op jit(solution)/shard_map/all_to_all | solution.py:230
  66.0 0.6 slice_bitcast_fusion
  (2 shorter events, 0.0 us)
Async XLA Ops:
  0.0 4.8 %copy-start = (bf16[4,256,512]{2,1,0:T(8,128)(2,1)S(1)}, bf16[4,256,512]{2,1,0:T(8,128)(2,1)}, u32[]{:S(2)}) copy-start(bf16[4,256,512]{2,1,0:T(8,128)(2,1)} %param.7) | copy-start | bytes 3145732
  0.0 3.5 %copy-start.3 = (bf16[64,1792]{1,0:T(8,128)(2,1)S(1)}, bf16[64,1792]{1,0:T(8,128)(2,1)}, u32[]{:S(2)}) copy-start(bf16[64,1792]{1,0:T(8,128)(2,1)} %param.10) | copy-start | bytes 688132
  0.0 3.5 %copy-start.1 = (bf16[4,256,1792]{2,1,0:T(8,128)(2,1)S(1)}, bf16[4,256,1792]{2,1,0:T(8,128)(2,1)}, u32[]{:S(2)}) copy-start(bf16[4,256,1792]{2,1,0:T(8,128)(2,1)} %param.8) | copy-start | bytes 11010052
  0.0 4.8 %copy-start.4 = (bf16[64,512]{1,0:T(8,128)(2,1)S(1)}, bf16[64,512]{1,0:T(8,128)(2,1)}, u32[]{:S(2)}) copy-start(bf16[64,512]{1,0:T(8,128)(2,1)} %param.11) | copy-start | bytes 196612
  3.6 1.7 %copy-start.2 = (bf16[4,256,512]{2,1,0:T(8,128)(2,1)S(1)}, bf16[4,256,512]{2,1,0:T(8,128)(2,1)}, u32[]{:S(2)}) copy-start(bf16[4,256,512]{2,1,0:T(8,128)(2,1)} %param.9) | copy-start | bytes 3145732
  5.8 4.9 %collective-permute-start = (f32[4,128,256]{2,1,0:T(8,128)S(1)}, f32[4,128,256]{2,1,0:T(8,128)S(1)}, u32[]{:S(2)}, u32[]{:S(2)}) collective-permute-start(f32[4,128,256]{2,1,0:T(8,128)S(1)} %select_bitcast_fusion), channel_id=1, source_target_pairs={{0,1},{1,0},{2,3},{3,2},{4,5},{5,4},{6,7},{7,6},{8,9},{9,8},{10,11... | collective-permute-start | bytes 1572872 | tf_op jit(solution)/shard_map/ppermute | solution.py:239
  54.6 3.1 %collective-permute-start.1 = (f32[32,128]{1,0:T(8,128)S(1)}, f32[32,128]{1,0:T(8,128)S(1)}, u32[]{:S(2)}, u32[]{:S(2)}) collective-permute-start(f32[32,128]{1,0:T(8,128)S(1)} %shard_map.66), channel_id=1, source_target_pairs={{0,1},{1,0},{2,3},{3,2},{4,5},{5,4},{6,7},{7,6},{8,9},{9,8},{10,11... | collective-permute-start | bytes 49160 | tf_op jit(solution)/shard_map/ppermute | solution.py:251

commit v4 on v3

--- a/solution.py
+++ b/solution.py
@@ -96,7 +96,7 @@
             for query in range(got.shape[0]):
                 tile = got[query, 8 * share : 8 * share + 8]
                 for column in range(4):
-                    send[column * 4 + share, 8 * query : 8 * query + 8] = tile
+                    send[share * 4 + column, 8 * query : 8 * query + 8] = tile
         for peer in range(send.shape[0]):
             send[peer, 64:72] = got[0, 32:40]
 
@@ -171,7 +171,7 @@
         share = pl.multiple_of(lax.axis_index("y") * 8, 8)
         inverse_out = jnp.concatenate([held[pl.ds(share, 8)], held[pl.ds(share + 32, 8)]], axis=0)
         halves = jnp.concatenate([inverse_out[:, :32], inverse_out[:, 32:RANK]], axis=0)
-        grads = jnp.concatenate([got[lax.axis_index("x") * 4 + seq, 40:72] for seq in range(4)], axis=1)
+        grads = jnp.concatenate([got[seq * 4 + lax.axis_index("x"), 40:72] for seq in range(4)], axis=1)
         products = jnp.dot(halves, grads, precision=HIGH, preferred_element_type=jnp.float32)
         lefts = []
         for seq in range(4):
@@ -195,26 +195,31 @@
         out[...] = jnp.zeros_like(out)
 
 
-def score_kernel(scale, got, ready, send):
-    tiles = []
-    for x in range(4):
-        for z in range(8):
-            for y in range(4):
-                tiles.append(got[x * 4 + y, 8 * z : 8 * z + 8])
-    queries = jnp.concatenate(tiles, axis=0)
-    high, low = split(queries)
-    both = jnp.concatenate(split(ready[...]), axis=0)
+def split_kernel(got, out):
+    @pl.when(lax.axis_index("c") != TRAIN_CORE)
+    def _():
+        for row in range(8):
+            tiles = [got[peer, pl.ds(row, 8, stride=8), :] for peer in range(got.shape[0])]
+            columns = slice(LANES * row, LANES * row + LANES)
+            out[0, :, columns], out[1, :, columns] = split(jnp.concatenate(tiles, axis=0))
+
+
+def score_kernel(scale, queries, ready, send):
+    tiles = ready[...].reshape(4, 8, LANES)
+    rows = [tiles[:, row, :] for row in range(8)]
+    trains = jnp.concatenate(rows, axis=1)
+    trains = jnp.concatenate([trains, trains], axis=0) * scale
+    high, low = split(trains)
+    high = high.astype(jnp.float32)
+    terms = jnp.where(iota(trains.shape, 0) < 4, high, low.astype(jnp.float32))
+    terms = terms.astype(jnp.bfloat16)
     dims = (((1,), (1,)), ((), ()))
-    pairs = lax.dot_general(high, both, dims, preferred_element_type=jnp.float32)
-    pairs += lax.dot_general(low, both, dims, preferred_element_type=jnp.float32)
-    pairs = pairs[:, :32] + pairs[:, 32:]
-    count = len(tiles)
-    same = (iota((8 * count, 32), 0) & 7) == (iota((8 * count, 32), 1) & 7)
-    sums = jnp.where(same, pairs, 0.0).reshape(count, 8, 32).sum(axis=1)
-    pick = jnp.where(iota((8, 32), 0) == iota((8, 32), 1) // 8, scale, 0.0)
-    scores = lax.dot_general(
-        pick, sums, (((1,), (1,)), ((), ())), precision=HIGH, preferred_element_type=jnp.float32
-    )
+    scores = lax.dot_general(terms, queries[0], dims, preferred_element_type=jnp.float32)
+    scores += lax.dot_general(terms, queries[1], dims, preferred_element_type=jnp.float32)
+    scores = scores + pltpu.roll(scores, 4, 0)
+    lane = iota(scores.shape, 1)
+    source = (lane & 3) * 32 + (lane >> 2)
+    scores = jnp.take_along_axis(scores, source, axis=1, mode="promise_in_bounds")
     for peer in range(send.shape[0]):
         send[peer] = scores
 
@@ -242,7 +247,7 @@
     send, own = call(gram_kernel, (f32(8, 40, LANES), f32(32, LANES)))(parts)
     got = swap(send, "z")
     send = call(spread_kernel, f32(16, 72, LANES))(got, own)
-    got = swap(send, ("x", "y"))
+    got = swap(send, ("y", "x"))
     ready = call(
         functools.partial(ready_kernel, total_tokens),
         f32(32, LANES),
@@ -250,9 +255,10 @@
     )(got)
     ready = lax.ppermute(ready, "c", [(0, 1), (1, 0)])
     scale = 1.0 / (seq_len * RANK)
-    send = call(functools.partial(score_kernel, scale), f32(8, 8, LANES))(got, ready)
-    got = swap(send, ("y", "c"))
-    return ((got[0] + got[2]) + (got[4] + got[6]))[:4]
+    queries = call(split_kernel, jax.ShapeDtypeStruct((2, LANES, 8 * LANES), jnp.bfloat16))(got)
+    send = call(functools.partial(score_kernel, scale), f32(8, 8, LANES))(queries, ready)
+    got = swap(send, ("c", "y"))
+    return ((got[0] + got[1]) + (got[2] + got[3]))[:4]
 
 
 def solution(mesh):

time: 66.8 us -> 66.4 us (level)
    pallas_call x4 -> x5, Pallas kernels: 3.48 us -> 3.01 us  [wrapped(): pl.pallas_call(body, out_shape=out, in_specs=[VM] * len(args), out_specs=...]
where the time goes in v4:
time: 66.4 us; the launch traced here: 66.2 us
  blocking collectives  48.8 us (73%)
  matrix products  5.58 us (8%)
  starting transfers between devices  5.58 us (8%)
  Pallas kernels  3.01 us (5%)
  waiting for transfers between devices  2.37 us (4%)
    all_to_all x4, blocking collectives, swap(): return lax.all_to_all(value, axis, 0, 0, tiled=True)  48.8 us
    dot_general x2, matrix products, features(): lax.dot_general(proj_in, acts, dims, preferred_element_type=jnp.float32)  4.72 us
    ppermute x1, starting transfers between devices, on_device(): lax.ppermute(jnp.where(is_train, query, train), 'c', [(0, 1), (1, 0)])  3.32 us
    pallas_call x5, Pallas kernels, wrapped(): pl.pallas_call(body, out_shape=out, in_specs=[VM] * len(args), out_specs=...  3.01 us
    ppermute x1, starting transfers between devices, on_device(): ready = lax.ppermute(ready, 'c', [(0, 1), (1, 0)])  2.27 us
    ppermute x1, waiting for transfers between devices, on_device(): lax.ppermute(jnp.where(is_train, query, train), 'c', [(0, 1), (1, 0)])  1.54 us
  transfers between devices with their start and end apart: 2, of which 2 were waited for; matrix products, arithmetic and copies ran while one was open for 0% of the time, Pallas kernels for 0%

profile of v4, /device:TPU:1, one launch (start us, length us, event | category | flops | bytes accessed | tf_op | source)
XLA Modules:
  0.0 66.2 jit_solution(10943041273702104208)
XLA Ops:
  0.0 0.0 copy-start
  0.0 0.0 copy-start.3
  0.0 0.0 copy-start.1
  0.0 0.0 copy-start.4
  0.0 3.5 %fusion.2 = f32[64,4,256]{2,0,1:T(8,128)S(1)} fusion(bf16[4,256,1792]{2,1,0:T(8,128)(2,1)} %param.6, bf16[64,1792]{1,0:T(8,128)(2,1)} %param.10), kind=kOutput, calls=%fused_computation.6 | convolution fusion | flops 234881024 | bytes 4161536 | tf_op jit(solution)/shard_map/dot_general | solution.py:229
  3.5 0.0 copy-done.3
  3.5 0.0 copy-done.1
  3.6 0.0 copy-start.2
  3.6 1.2 %fusion = f32[64,4,256]{2,0,1:T(8,128)S(1)} fusion(bf16[4,256,1792]{2,1,0:T(8,128)(2,1)S(1)} %copy-done.1, bf16[64,1792]{1,0:T(8,128)(2,1)S(1)} %copy-done.3), kind=kOutput, calls=%fused_computation.4 | convolution fusion | flops 234881024 | bytes 4161536 | tf_op jit(solution)/shard_map/dot_general | solution.py:229
  4.8 0.0 copy-done
  4.8 0.0 copy-done.4
  4.8 0.4 fusion.6
  5.2 0.0 copy-done.2
  5.2 0.4 fusion.4
  5.7 0.1 select_bitcast_fusion
  5.8 3.3 %collective-permute-start = (f32[4,128,256]{2,1,0:T(8,128)S(1)}, f32[4,128,256]{2,1,0:T(8,128)S(1)}, u32[]{:S(2)}, u32[]{:S(2)}) collective-permute-start(f32[4,128,256]{2,1,0:T(8,128)S(1)} %select_bitcast_fusion), channel_id=1, source_target_pairs={{0,1},{1,0},{2,3},{3,2},{4,5},{5,4},{6,7},{7,6},{8,9},{9,8},{10,11... | collective-permute-start | bytes 1572872 | tf_op jit(solution)/shard_map/ppermute | solution.py:244
  9.1 1.5 %collective-permute-done = f32[4,128,256]{2,1,0:T(8,128)S(1)} collective-permute-done((f32[4,128,256]{2,1,0:T(8,128)S(1)}, f32[4,128,256]{2,1,0:T(8,128)S(1)}, u32[]{:S(2)}, u32[]{:S(2)}) %collective-permute-start) | collective-permute-done | bytes 524320 | tf_op jit(solution)/shard_map/ppermute | solution.py:244
  10.6 0.1 bitcast_add_fusion
  10.7 11.5 %all_to_all.20.parts = f32[4,128,256]{2,1,0:T(8,128)S(1)} all-to-all(f32[4,128,256]{2,1,0:T(8,128)S(1)} %bitcast_add_fusion), channel_id=1, replica_groups=mesh['x'=4,'z'=8,'y'=4,'c'=2] {'y'}, dimensions={0} | all-to-all | bytes 1048576 | tf_op jit(solution)/shard_map/all_to_all | solution.py:235
  22.2 0.4 shard_map.64
  22.6 15.8 %all_to_all.21.got = f32[8,40,128]{2,1,0:T(8,128)S(1)} all-to-all(f32[8,40,128]{2,1,0:T(8,128)S(1)} %get-tuple-element.7), channel_id=1, replica_groups=mesh['x'=4,'z'=8,'y'=4,'c'=2] {'z'}, dimensions={0} | all-to-all | bytes 327680 | tf_op jit(solution)/shard_map/all_to_all | solution.py:235
  38.4 13.9 %all_to_all.22.got = f32[16,72,128]{2,1,0:T(8,128)S(1)} all-to-all(f32[16,72,128]{2,1,0:T(8,128)S(1)} %shard_map.65), channel_id=1, replica_groups=mesh['x'=4,'z'=8,'y'=4,'c'=2] {'y','x'}, dimensions={0} | all-to-all | bytes 1179648 | tf_op jit(solution)/shard_map/all_to_all | solution.py:235
  52.3 2.3 %shard_map.67 = f32[32,128]{1,0:T(8,128)S(1)} custom-call(f32[16,72,128]{2,1,0:T(8,128)S(1)} %all_to_all.22.got), custom_call_target="tpu_custom_call" | custom-call | tf_op jit(solution)/shard_map/pallas_call | solution.py:23
  54.6 2.3 %collective-permute-start.1 = (f32[32,128]{1,0:T(8,128)S(1)}, f32[32,128]{1,0:T(8,128)S(1)}, u32[]{:S(2)}, u32[]{:S(2)}) collective-permute-start(f32[32,128]{1,0:T(8,128)S(1)} %shard_map.67), channel_id=1, source_target_pairs={{0,1},{1,0},{2,3},{3,2},{4,5},{5,4},{6,7},{7,6},{8,9},{9,8},{10,11... | collective-permute-start | bytes 49160 | tf_op jit(solution)/shard_map/ppermute | solution.py:256
  56.9 0.8 %collective-permute-done.1.ready = f32[32,128]{1,0:T(8,128)S(1)} collective-permute-done((f32[32,128]{1,0:T(8,128)S(1)}, f32[32,128]{1,0:T(8,128)S(1)}, u32[]{:S(2)}, u32[]{:S(2)}) %collective-permute-start.1) | collective-permute-done | bytes 16416 | tf_op jit(solution)/shard_map/ppermute | solution.py:256
  57.7 0.3 shard_map.68
  58.0 7.6 %all_to_all.23 = f32[8,8,128]{2,1,0:T(8,128)S(1)} all-to-all(f32[8,8,128]{2,1,0:T(8,128)S(1)} %shard_map.68), channel_id=1, replica_groups=mesh['x'=4,'z'=8,'y'=4,'c'=2] {'c','y'}, dimensions={0} | all-to-all | bytes 65536 | tf_op jit(solution)/shard_map/all_to_all | solution.py:235
  65.6 0.6 slice_bitcast_fusion
  (3 shorter events, 0.1 us)
Async XLA Ops:
  0.0 4.8 %copy-start = (bf16[4,256,512]{2,1,0:T(8,128)(2,1)S(1)}, bf16[4,256,512]{2,1,0:T(8,128)(2,1)}, u32[]{:S(2)}) copy-start(bf16[4,256,512]{2,1,0:T(8,128)(2,1)} %param.7) | copy-start | bytes 3145732
  0.0 3.5 %copy-start.3 = (bf16[64,1792]{1,0:T(8,128)(2,1)S(1)}, bf16[64,1792]{1,0:T(8,128)(2,1)}, u32[]{:S(2)}) copy-start(bf16[64,1792]{1,0:T(8,128)(2,1)} %param.10) | copy-start | bytes 688132
  0.0 3.5 %copy-start.1 = (bf16[4,256,1792]{2,1,0:T(8,128)(2,1)S(1)}, bf16[4,256,1792]{2,1,0:T(8,128)(2,1)}, u32[]{:S(2)}) copy-start(bf16[4,256,1792]{2,1,0:T(8,128)(2,1)} %param.8) | copy-start | bytes 11010052
  0.0 4.8 %copy-start.4 = (bf16[64,512]{1,0:T(8,128)(2,1)S(1)}, bf16[64,512]{1,0:T(8,128)(2,1)}, u32[]{:S(2)}) copy-start(bf16[64,512]{1,0:T(8,128)(2,1)} %param.11) | copy-start | bytes 196612
  3.6 1.7 %copy-start.2 = (bf16[4,256,512]{2,1,0:T(8,128)(2,1)S(1)}, bf16[4,256,512]{2,1,0:T(8,128)(2,1)}, u32[]{:S(2)}) copy-start(bf16[4,256,512]{2,1,0:T(8,128)(2,1)} %param.9) | copy-start | bytes 3145732
  5.8 4.9 %collective-permute-start = (f32[4,128,256]{2,1,0:T(8,128)S(1)}, f32[4,128,256]{2,1,0:T(8,128)S(1)}, u32[]{:S(2)}, u32[]{:S(2)}) collective-permute-start(f32[4,128,256]{2,1,0:T(8,128)S(1)} %select_bitcast_fusion), channel_id=1, source_target_pairs={{0,1},{1,0},{2,3},{3,2},{4,5},{5,4},{6,7},{7,6},{8,9},{9,8},{10,11... | collective-permute-start | bytes 1572872 | tf_op jit(solution)/shard_map/ppermute | solution.py:244
  54.6 3.1 %collective-permute-start.1 = (f32[32,128]{1,0:T(8,128)S(1)}, f32[32,128]{1,0:T(8,128)S(1)}, u32[]{:S(2)}, u32[]{:S(2)}) collective-permute-start(f32[32,128]{1,0:T(8,128)S(1)} %shard_map.67), channel_id=1, source_target_pairs={{0,1},{1,0},{2,3},{3,2},{4,5},{5,4},{6,7},{7,6},{8,9},{9,8},{10,11... | collective-permute-start | bytes 49160 | tf_op jit(solution)/shard_map/ppermute | solution.py:256

commit v5 on v4

--- a/solution.py
+++ b/solution.py
@@ -50,18 +50,19 @@
 
 
 def split(value):
-    high = value.astype(jnp.bfloat16)
-    return high, (value - high.astype(jnp.float32)).astype(jnp.bfloat16)
+    terms = []
+    for _ in range(3):
+        term = value.astype(jnp.bfloat16)
+        terms.append(term)
+        value = value - term.astype(jnp.float32)
+    return terms
 
 
 def gram_kernel(parts, send, own):
     total = (parts[0] + parts[1]) + (parts[2] + parts[3])
-    terms = jnp.concatenate(split(total), axis=0)
-    grams = lax.dot_general(
-        terms, terms, (((1,), (1,)), ((), ())), preferred_element_type=jnp.float32
+    gram = lax.dot_general(
+        total, total, (((1,), (1,)), ((), ())), precision=HIGH, preferred_element_type=jnp.float32
     )
-    high, low = grams[:LANES], grams[LANES:]
-    gram = high[:, :LANES] + ((high[:, LANES:] + low[:, :LANES]) + low[:, LANES:])
     top = gram[:RANK]
     low = gram[RANK:]
     side_out = pltpu.roll(low, RANK, 1)
@@ -201,21 +202,25 @@
         for row in range(8):
             tiles = [got[peer, pl.ds(row, 8, stride=8), :] for peer in range(got.shape[0])]
             columns = slice(LANES * row, LANES * row + LANES)
-            out[0, :, columns], out[1, :, columns] = split(jnp.concatenate(tiles, axis=0))
+            for index, term in enumerate(split(jnp.concatenate(tiles, axis=0))):
+                out[index, :, columns] = term
 
 
 def score_kernel(scale, queries, ready, send):
     tiles = ready[...].reshape(4, 8, LANES)
     rows = [tiles[:, row, :] for row in range(8)]
     trains = jnp.concatenate(rows, axis=1)
-    trains = jnp.concatenate([trains, trains], axis=0) * scale
-    high, low = split(trains)
-    high = high.astype(jnp.float32)
-    terms = jnp.where(iota(trains.shape, 0) < 4, high, low.astype(jnp.float32))
+    trains = jnp.concatenate([trains] * 4, axis=0) * scale
+    group = iota(trains.shape, 0) // 4
+    terms = jnp.zeros_like(trains)
+    for index, term in enumerate(split(trains)):
+        terms = jnp.where(group == index, term.astype(jnp.float32), terms)
     terms = terms.astype(jnp.bfloat16)
     dims = (((1,), (1,)), ((), ()))
-    scores = lax.dot_general(terms, queries[0], dims, preferred_element_type=jnp.float32)
-    scores += lax.dot_general(terms, queries[1], dims, preferred_element_type=jnp.float32)
+    scores = jnp.zeros((16, queries.shape[1]), jnp.float32)
+    for index in range(queries.shape[0]):
+        scores += lax.dot_general(terms, queries[index], dims, preferred_element_type=jnp.float32)
+    scores = scores[:8] + scores[8:]
     scores = scores + pltpu.roll(scores, 4, 0)
     lane = iota(scores.shape, 1)
     source = (lane & 3) * 32 + (lane >> 2)
@@ -255,7 +260,7 @@
     )(got)
     ready = lax.ppermute(ready, "c", [(0, 1), (1, 0)])
     scale = 1.0 / (seq_len * RANK)
-    queries = call(split_kernel, jax.ShapeDtypeStruct((2, LANES, 8 * LANES), jnp.bfloat16))(got)
+    queries = call(split_kernel, jax.ShapeDtypeStruct((3, LANES, 8 * LANES), jnp.bfloat16))(got)
     send = call(functools.partial(score_kernel, scale), f32(8, 8, LANES))(queries, ready)
     got = swap(send, ("c", "y"))
     return ((got[0] + got[1]) + (got[2] + got[3]))[:4]

time: 66.4 us -> 66.6 us (level)
  no operation moved by 1% of the time
where the time goes in v5:
time: 66.6 us; the launch traced here: 66.3 us
  blocking collectives  48.8 us (73%)
  matrix products  5.58 us (8%)
  starting transfers between devices  5.58 us (8%)
  Pallas kernels  3.12 us (5%)
  waiting for transfers between devices  2.37 us (4%)
    all_to_all x4, blocking collectives, swap(): return lax.all_to_all(value, axis, 0, 0, tiled=True)  48.8 us
    dot_general x2, matrix products, features(): lax.dot_general(proj_in, acts, dims, preferred_element_type=jnp.float32)  4.72 us
    ppermute x1, starting transfers between devices, on_device(): lax.ppermute(jnp.where(is_train, query, train), 'c', [(0, 1), (1, 0)])  3.32 us
    pallas_call x5, Pallas kernels, wrapped(): pl.pallas_call(body, out_shape=out, in_specs=[VM] * len(args), out_specs=...  3.12 us
    ppermute x1, starting transfers between devices, on_device(): ready = lax.ppermute(ready, 'c', [(0, 1), (1, 0)])  2.27 us
    ppermute x1, waiting for transfers between devices, on_device(): lax.ppermute(jnp.where(is_train, query, train), 'c', [(0, 1), (1, 0)])  1.54 us
  transfers between devices with their start and end apart: 2, of which 2 were waited for; matrix products, arithmetic and copies ran while one was open for 0% of the time, Pallas kernels for 0%

profile of v5, /device:TPU:1, one launch (start us, length us, event | category | flops | bytes accessed | tf_op | source)
XLA Modules:
  0.0 66.3 jit_solution(10127540240527828815)
XLA Ops:
  0.0 0.0 copy-start
  0.0 0.0 copy-start.3
  0.0 0.0 copy-start.1
  0.0 0.0 copy-start.4
  0.0 3.5 %fusion.2 = f32[64,4,256]{2,0,1:T(8,128)S(1)} fusion(bf16[4,256,1792]{2,1,0:T(8,128)(2,1)} %param.6, bf16[64,1792]{1,0:T(8,128)(2,1)} %param.10), kind=kOutput, calls=%fused_computation.6 | convolution fusion | flops 234881024 | bytes 4161536 | tf_op jit(solution)/shard_map/dot_general | solution.py:234
  3.5 0.0 copy-done.3
  3.5 0.0 copy-done.1
  3.6 0.0 copy-start.2
  3.6 1.2 %fusion = f32[64,4,256]{2,0,1:T(8,128)S(1)} fusion(bf16[4,256,1792]{2,1,0:T(8,128)(2,1)S(1)} %copy-done.1, bf16[64,1792]{1,0:T(8,128)(2,1)S(1)} %copy-done.3), kind=kOutput, calls=%fused_computation.4 | convolution fusion | flops 234881024 | bytes 4161536 | tf_op jit(solution)/shard_map/dot_general | solution.py:234
  4.8 0.0 copy-done
  4.8 0.0 copy-done.4
  4.8 0.4 fusion.6
  5.2 0.0 copy-done.2
  5.2 0.4 fusion.4
  5.7 0.1 select_bitcast_fusion
  5.8 3.3 %collective-permute-start = (f32[4,128,256]{2,1,0:T(8,128)S(1)}, f32[4,128,256]{2,1,0:T(8,128)S(1)}, u32[]{:S(2)}, u32[]{:S(2)}) collective-permute-start(f32[4,128,256]{2,1,0:T(8,128)S(1)} %select_bitcast_fusion), channel_id=1, source_target_pairs={{0,1},{1,0},{2,3},{3,2},{4,5},{5,4},{6,7},{7,6},{8,9},{9,8},{10,11... | collective-permute-start | bytes 1572872 | tf_op jit(solution)/shard_map/ppermute | solution.py:249
  9.1 1.5 %collective-permute-done = f32[4,128,256]{2,1,0:T(8,128)S(1)} collective-permute-done((f32[4,128,256]{2,1,0:T(8,128)S(1)}, f32[4,128,256]{2,1,0:T(8,128)S(1)}, u32[]{:S(2)}, u32[]{:S(2)}) %collective-permute-start) | collective-permute-done | bytes 524320 | tf_op jit(solution)/shard_map/ppermute | solution.py:249
  10.6 0.1 bitcast_add_fusion
  10.7 11.5 %all_to_all.20.parts = f32[4,128,256]{2,1,0:T(8,128)S(1)} all-to-all(f32[4,128,256]{2,1,0:T(8,128)S(1)} %bitcast_add_fusion), channel_id=1, replica_groups=mesh['x'=4,'z'=8,'y'=4,'c'=2] {'y'}, dimensions={0} | all-to-all | bytes 1048576 | tf_op jit(solution)/shard_map/all_to_all | solution.py:240
  22.2 0.4 shard_map.64
  22.6 15.8 %all_to_all.21.got = f32[8,40,128]{2,1,0:T(8,128)S(1)} all-to-all(f32[8,40,128]{2,1,0:T(8,128)S(1)} %get-tuple-element.7), channel_id=1, replica_groups=mesh['x'=4,'z'=8,'y'=4,'c'=2] {'z'}, dimensions={0} | all-to-all | bytes 327680 | tf_op jit(solution)/shard_map/all_to_all | solution.py:240
  38.4 13.9 %all_to_all.22.got = f32[16,72,128]{2,1,0:T(8,128)S(1)} all-to-all(f32[16,72,128]{2,1,0:T(8,128)S(1)} %shard_map.65), channel_id=1, replica_groups=mesh['x'=4,'z'=8,'y'=4,'c'=2] {'y','x'}, dimensions={0} | all-to-all | bytes 1179648 | tf_op jit(solution)/shard_map/all_to_all | solution.py:240
  52.3 2.3 %shard_map.67 = f32[32,128]{1,0:T(8,128)S(1)} custom-call(f32[16,72,128]{2,1,0:T(8,128)S(1)} %all_to_all.22.got), custom_call_target="tpu_custom_call" | custom-call | tf_op jit(solution)/shard_map/pallas_call | solution.py:23
  54.6 2.3 %collective-permute-start.1 = (f32[32,128]{1,0:T(8,128)S(1)}, f32[32,128]{1,0:T(8,128)S(1)}, u32[]{:S(2)}, u32[]{:S(2)}) collective-permute-start(f32[32,128]{1,0:T(8,128)S(1)} %shard_map.67), channel_id=1, source_target_pairs={{0,1},{1,0},{2,3},{3,2},{4,5},{5,4},{6,7},{7,6},{8,9},{9,8},{10,11... | collective-permute-start | bytes 49160 | tf_op jit(solution)/shard_map/ppermute | solution.py:261
  56.9 0.8 %collective-permute-done.1.ready = f32[32,128]{1,0:T(8,128)S(1)} collective-permute-done((f32[32,128]{1,0:T(8,128)S(1)}, f32[32,128]{1,0:T(8,128)S(1)}, u32[]{:S(2)}, u32[]{:S(2)}) %collective-permute-start.1) | collective-permute-done | bytes 16416 | tf_op jit(solution)/shard_map/ppermute | solution.py:261
  57.7 0.4 shard_map.68
  58.1 7.6 %all_to_all.23 = f32[8,8,128]{2,1,0:T(8,128)S(1)} all-to-all(f32[8,8,128]{2,1,0:T(8,128)S(1)} %shard_map.68), channel_id=1, replica_groups=mesh['x'=4,'z'=8,'y'=4,'c'=2] {'c','y'}, dimensions={0} | all-to-all | bytes 65536 | tf_op jit(solution)/shard_map/all_to_all | solution.py:240
  65.8 0.6 slice_bitcast_fusion
  (3 shorter events, 0.1 us)
Async XLA Ops:
  0.0 4.8 %copy-start = (bf16[4,256,512]{2,1,0:T(8,128)(2,1)S(1)}, bf16[4,256,512]{2,1,0:T(8,128)(2,1)}, u32[]{:S(2)}) copy-start(bf16[4,256,512]{2,1,0:T(8,128)(2,1)} %param.7) | copy-start | bytes 3145732
  0.0 3.5 %copy-start.3 = (bf16[64,1792]{1,0:T(8,128)(2,1)S(1)}, bf16[64,1792]{1,0:T(8,128)(2,1)}, u32[]{:S(2)}) copy-start(bf16[64,1792]{1,0:T(8,128)(2,1)} %param.10) | copy-start | bytes 688132
  0.0 3.5 %copy-start.1 = (bf16[4,256,1792]{2,1,0:T(8,128)(2,1)S(1)}, bf16[4,256,1792]{2,1,0:T(8,128)(2,1)}, u32[]{:S(2)}) copy-start(bf16[4,256,1792]{2,1,0:T(8,128)(2,1)} %param.8) | copy-start | bytes 11010052
  0.0 4.8 %copy-start.4 = (bf16[64,512]{1,0:T(8,128)(2,1)S(1)}, bf16[64,512]{1,0:T(8,128)(2,1)}, u32[]{:S(2)}) copy-start(bf16[64,512]{1,0:T(8,128)(2,1)} %param.11) | copy-start | bytes 196612
  3.6 1.7 %copy-start.2 = (bf16[4,256,512]{2,1,0:T(8,128)(2,1)S(1)}, bf16[4,256,512]{2,1,0:T(8,128)(2,1)}, u32[]{:S(2)}) copy-start(bf16[4,256,512]{2,1,0:T(8,128)(2,1)} %param.9) | copy-start | bytes 3145732
  5.8 4.9 %collective-permute-start = (f32[4,128,256]{2,1,0:T(8,128)S(1)}, f32[4,128,256]{2,1,0:T(8,128)S(1)}, u32[]{:S(2)}, u32[]{:S(2)}) collective-permute-start(f32[4,128,256]{2,1,0:T(8,128)S(1)} %select_bitcast_fusion), channel_id=1, source_target_pairs={{0,1},{1,0},{2,3},{3,2},{4,5},{5,4},{6,7},{7,6},{8,9},{9,8},{10,11... | collective-permute-start | bytes 1572872 | tf_op jit(solution)/shard_map/ppermute | solution.py:249
  54.6 3.1 %collective-permute-start.1 = (f32[32,128]{1,0:T(8,128)S(1)}, f32[32,128]{1,0:T(8,128)S(1)}, u32[]{:S(2)}, u32[]{:S(2)}) collective-permute-start(f32[32,128]{1,0:T(8,128)S(1)} %shard_map.67), channel_id=1, source_target_pairs={{0,1},{1,0},{2,3},{3,2},{4,5},{5,4},{6,7},{7,6},{8,9},{9,8},{10,11... | collective-permute-start | bytes 49160 | tf_op jit(solution)/shard_map/ppermute | solution.py:261

commit v6 on v5

--- a/solution.py
+++ b/solution.py
@@ -60,24 +60,35 @@
 
 def gram_kernel(parts, send, own):
     total = (parts[0] + parts[1]) + (parts[2] + parts[3])
-    gram = lax.dot_general(
-        total, total, (((1,), (1,)), ((), ())), precision=HIGH, preferred_element_type=jnp.float32
-    )
-    top = gram[:RANK]
-    low = gram[RANK:]
-    side_out = pltpu.roll(low, RANK, 1)
-    row = iota((RANK, LANES), 0)
-    lane = iota((RANK, LANES), 1)
-    both = pack(jnp.where(row <= lane, top, side_out))
-    diag = jnp.sum(jnp.where(row == lane, side_out, 0.0), axis=0, keepdims=True)
-    grad = pack(low)
-    own[...] = grad
-    is_train = lax.axis_index("c") == TRAIN_CORE
-    first = jnp.where(is_train, both, grad)
-    rest = jnp.broadcast_to(diag, (8, LANES))
-    for peer in range(send.shape[0]):
-        send[peer, :32] = first
-        send[peer, 32:40] = rest
+    dims = (((1,), (1,)), ((), ()))
+
+    @pl.when(lax.axis_index("c") == TRAIN_CORE)
+    def _():
+        gram = lax.dot_general(
+            total, total, dims, precision=HIGH, preferred_element_type=jnp.float32
+        )
+        low = gram[RANK:]
+        side_out = pltpu.roll(low, RANK, 1)
+        row = iota((RANK, LANES), 0)
+        lane = iota((RANK, LANES), 1)
+        both = pack(jnp.where(row <= lane, gram[:RANK], side_out))
+        diag = jnp.sum(jnp.where(row == lane, side_out, 0.0), axis=0, keepdims=True)
+        own[...] = pack(low)
+        rest = jnp.broadcast_to(diag, (8, LANES))
+        for peer in range(send.shape[0]):
+            send[peer, :32] = both
+            send[peer, 32:40] = rest
+
+    @pl.when(lax.axis_index("c") != TRAIN_CORE)
+    def _():
+        low = lax.dot_general(
+            total[RANK:], total, dims, precision=HIGH, preferred_element_type=jnp.float32
+        )
+        grad = pack(low)
+        own[...] = grad
+        for peer in range(send.shape[0]):
+            send[peer, :32] = grad
+            send[peer, 32:40] = grad[:8]
 
 
 def spread_kernel(got, own, send):
@@ -207,33 +218,38 @@
 
 
 def score_kernel(scale, queries, ready, send):
-    tiles = ready[...].reshape(4, 8, LANES)
-    rows = [tiles[:, row, :] for row in range(8)]
-    trains = jnp.concatenate(rows, axis=1)
-    trains = jnp.concatenate([trains] * 4, axis=0) * scale
-    group = iota(trains.shape, 0) // 4
-    terms = jnp.zeros_like(trains)
-    for index, term in enumerate(split(trains)):
-        terms = jnp.where(group == index, term.astype(jnp.float32), terms)
-    terms = terms.astype(jnp.bfloat16)
-    dims = (((1,), (1,)), ((), ()))
-    scores = jnp.zeros((16, queries.shape[1]), jnp.float32)
-    for index in range(queries.shape[0]):
-        scores += lax.dot_general(terms, queries[index], dims, preferred_element_type=jnp.float32)
-    scores = scores[:8] + scores[8:]
-    scores = scores + pltpu.roll(scores, 4, 0)
-    lane = iota(scores.shape, 1)
-    source = (lane & 3) * 32 + (lane >> 2)
-    scores = jnp.take_along_axis(scores, source, axis=1, mode="promise_in_bounds")
-    for peer in range(send.shape[0]):
-        send[peer] = scores
-
-
-def features(acts, grads, proj_in, proj_out):
-    dims = (((1,), (2,)), ((), ()))
-    feat_in = lax.dot_general(proj_in, acts, dims, preferred_element_type=jnp.float32)
-    feat_out = lax.dot_general(proj_out, grads, dims, preferred_element_type=jnp.float32)
-    return jnp.concatenate([feat_in, feat_out], axis=0).transpose(1, 0, 2)
+    @pl.when(lax.axis_index("c") != TRAIN_CORE)
+    def _():
+        tiles = ready[...].reshape(4, 8, LANES)
+        rows = [tiles[:, row, :] for row in range(8)]
+        trains = jnp.concatenate(rows, axis=1)
+        trains = jnp.concatenate([trains] * 4, axis=0) * scale
+        group = iota(trains.shape, 0) // 4
+        terms = jnp.zeros_like(trains)
+        for index, term in enumerate(split(trains)):
+            terms = jnp.where(group == index, term.astype(jnp.float32), terms)
+        terms = terms.astype(jnp.bfloat16)
+        dims = (((1,), (1,)), ((), ()))
+        scores = jnp.zeros((16, queries.shape[1]), jnp.float32)
+        for index in range(queries.shape[0]):
+            scores += lax.dot_general(terms, queries[index], dims, preferred_element_type=jnp.float32)
+        scores = scores[:8] + scores[8:]
+        scores = scores + pltpu.roll(scores, 4, 0)
+        lane = iota(scores.shape, 1)
+        source = (lane & 3) * 32 + (lane >> 2)
+        scores = jnp.take_along_axis(scores, source, axis=1, mode="promise_in_bounds")
+        for peer in range(send.shape[0]):
+            send[peer] = scores
+
+    @pl.when(lax.axis_index("c") == TRAIN_CORE)
+    def _():
+        send[...] = jnp.zeros_like(send)
+
+
+def product(weight, rows):
+    return lax.dot_general(
+        weight, rows, (((1,), (2,)), ((), ())), preferred_element_type=jnp.float32
+    ).transpose(1, 0, 2)
 
 
 def swap(value, axis):
@@ -244,10 +260,20 @@
     seq_len = train_acts.shape[1]
     total_tokens = train_acts.shape[0] * seq_len * 32
     is_train = lax.axis_index("c") == TRAIN_CORE
-    train = features(train_acts, train_grads, proj_in, proj_out)
-    query = features(query_acts, query_grads, proj_in, proj_out)
-    other = lax.ppermute(jnp.where(is_train, query, train), "c", [(0, 1), (1, 0)])
-    mine = jnp.where(is_train, train, query) + other
+    flip = [(0, 1), (1, 0)]
+    train_in = product(proj_in, train_acts)
+    query_in = product(proj_in, query_acts)
+    other_in = jnp.where(is_train, query_in, train_in)
+    proj_out, other_in = lax.optimization_barrier((proj_out, other_in))
+    other_in = lax.ppermute(other_in, "c", flip)
+    train_out = product(proj_out, train_grads)
+    query_out = product(proj_out, query_grads)
+    other_out = lax.ppermute(jnp.where(is_train, query_out, train_out), "c", flip)
+    mine = jnp.where(
+        is_train,
+        jnp.concatenate([train_in, train_out], axis=1),
+        jnp.concatenate([query_in, query_out], axis=1),
+    ) + jnp.concatenate([other_in, other_out], axis=1)
     parts = swap(mine, "y")
     send, own = call(gram_kernel, (f32(8, 40, LANES), f32(32, LANES)))(parts)
     got = swap(send, "z")

time: 66.6 us -> 66.5 us (level)
  blocking collectives: 48.8 us -> 50 us
  starting transfers between devices: 5.58 us -> 4.71 us
    all_to_all x4, blocking collectives: 48.8 us -> 50 us  [swap(): return lax.all_to_all(value, axis, 0, 0, tiled=True)]
    ppermute x1, starting transfers between devices: 2.27 us -> 1.27 us  [on_device(): ready = lax.ppermute(ready, 'c', [(0, 1), (1, 0)])]
    ppermute x1 -> x2, starting transfers between devices: 3.32 us -> 3.43 us  [the longest x1 3.32 us: on_device(): other_in = lax.ppermute(other_in, 'c', flip)]
    ppermute x1 -> x2, waiting for transfers between devices: 1.54 us -> 1.5 us  [the longest x1 1.35 us: on_device(): lax.ppermute(jnp.where(is_train, query_out, train_out), 'c', flip)]
  transfers between devices with their start and end apart: 2 -> 3, of which waited for: 2 -> 3; matrix products, arithmetic and copies ran while one was open for 0% -> 1% of each run, Pallas kernels for 0% -> 0%
where the time goes in v6:
time: 66.5 us; the launch traced here: 66.2 us
  blocking collectives  50 us (75%)
  matrix products  5.6 us (8%)
  starting transfers between devices  4.71 us (7%)
  Pallas kernels  2.79 us (4%)
  waiting for transfers between devices  2.34 us (4%)
    all_to_all x4, blocking collectives, swap(): return lax.all_to_all(value, axis, 0, 0, tiled=True)  50 us
    dot_general x4, matrix products, product(): lax.dot_general(weight, rows, (((1,), (2,)), ((), ())), preferred_element...  5.6 us
    ppermute x1, starting transfers between devices, on_device(): other_in = lax.ppermute(other_in, 'c', flip)  3.32 us
    pallas_call x5, Pallas kernels, wrapped(): pl.pallas_call(body, out_shape=out, in_specs=[VM] * len(args), out_specs=...  2.79 us
    ppermute x1, waiting for transfers between devices, on_device(): lax.ppermute(jnp.where(is_train, query_out, train_out), 'c', flip)  1.35 us
  transfers between devices with their start and end apart: 3, of which 3 were waited for; matrix products, arithmetic and copies ran while one was open for 1% of the time, Pallas kernels for 0%

profile of v6, /device:TPU:1, one launch (start us, length us, event | category | flops | bytes accessed | tf_op | source)
XLA Modules:
  0.0 66.2 jit_solution(14535259744267493191)
XLA Ops:
  0.0 0.0 copy-start
  0.0 0.0 copy-start.3
  0.0 0.0 copy-start.1
  0.0 0.0 copy-start.2
  0.0 0.0 copy-start.4
  0.0 3.5 %convolution_bitcast_fusion.3 = f32[4,64,256]{2,1,0:T(8,128)S(1)} fusion(bf16[4,256,1792]{2,1,0:T(8,128)(2,1)} %param.6, bf16[64,1792]{1,0:T(8,128)(2,1)} %param.10), kind=kOutput, calls=%fused_computation.3 | convolution fusion | flops 234881024 | bytes 4161536 | tf_op jit(solution)/shard_map/dot_general | solution.py:250
  3.5 0.0 copy-done.3
  3.6 0.0 copy-done.1
  3.6 1.2 %broadcast_select_fusion.1 = (f32[4,64,256]{2,1,0:T(8,128)S(1)}, f32[4,64,256]{2,1,0:T(8,128)S(1)}) fusion(f32[4,64,256]{2,1,0:T(8,128)S(1)} %convolution_bitcast_fusion.3, pred[]{:T(512)S(6)} %eq.3, bf16[4,256,1792]{2,1,0:T(8,128)(2,1)S(1)} %copy-done.1, bf16[64,1792]{1,0:T(8,128)(2,1)S(1)} %copy-done.3), kind=kOutput, calls=%fused_computation.9 | convolution fusion | flops 234946560 | bytes 4685825 | tf_op jit(solution)/shard_map/dot_general | solution.py:250
  4.8 3.3 %collective-permute-start = (f32[4,64,256]{2,1,0:T(8,128)S(1)}, f32[4,64,256]{2,1,0:T(8,128)S(1)}, u32[]{:S(2)}, u32[]{:S(2)}) collective-permute-start(f32[4,64,256]{2,1,0:T(8,128)S(1)} %get-tuple-element.10), channel_id=1, source_target_pairs={{0,1},{1,0},{2,3},{3,2},{4,5},{5,4},{6,7},{7,6},{8,9},{9,8},{10,11... | collective-permute-start | bytes 786440 | tf_op jit(solution)/shard_map/ppermute | solution.py:268
  8.1 0.0 copy-done.2
  8.1 0.0 copy-done.4
  8.1 0.4 convolution_bitcast_fusion.1
  8.5 0.0 copy-done
  8.6 0.4 broadcast_select_fusion
  9.0 0.1 collective-permute-start.1
  9.1 0.2 collective-permute-done
  9.3 1.3 %collective-permute-done.1 = f32[4,64,256]{2,1,0:T(8,128)S(1)} collective-permute-done((f32[4,64,256]{2,1,0:T(8,128)S(1)}, f32[4,64,256]{2,1,0:T(8,128)S(1)}, u32[]{:S(2)}, u32[]{:S(2)}) %collective-permute-start.1) | collective-permute-done | bytes 262176 | tf_op jit(solution)/shard_map/ppermute | solution.py:271
  10.6 0.1 fusion
  10.7 11.7 %all_to_all.20.parts = f32[4,128,256]{2,1,0:T(8,128)S(1)} all-to-all(f32[4,128,256]{2,1,0:T(8,128)S(1)} %fusion), channel_id=1, replica_groups=mesh['x'=4,'z'=8,'y'=4,'c'=2] {'y'}, dimensions={0} | all-to-all | bytes 1048576 | tf_op jit(solution)/shard_map/all_to_all | solution.py:256
  22.5 0.4 shard_map.64
  22.9 16.0 %all_to_all.21.got = f32[8,40,128]{2,1,0:T(8,128)S(1)} all-to-all(f32[8,40,128]{2,1,0:T(8,128)S(1)} %get-tuple-element.11), channel_id=1, replica_groups=mesh['x'=4,'z'=8,'y'=4,'c'=2] {'z'}, dimensions={0} | all-to-all | bytes 327680 | tf_op jit(solution)/shard_map/all_to_all | solution.py:256
  39.0 14.3 %all_to_all.22.got = f32[16,72,128]{2,1,0:T(8,128)S(1)} all-to-all(f32[16,72,128]{2,1,0:T(8,128)S(1)} %shard_map.65), channel_id=1, replica_groups=mesh['x'=4,'z'=8,'y'=4,'c'=2] {'y','x'}, dimensions={0} | all-to-all | bytes 1179648 | tf_op jit(solution)/shard_map/all_to_all | solution.py:256
  53.2 2.3 %shard_map.67 = f32[32,128]{1,0:T(8,128)S(1)} custom-call(f32[16,72,128]{2,1,0:T(8,128)S(1)} %all_to_all.22.got), custom_call_target="tpu_custom_call" | custom-call | tf_op jit(solution)/shard_map/pallas_call | solution.py:23
  55.5 1.3 %collective-permute-start.2 = (f32[32,128]{1,0:T(8,128)S(1)}, f32[32,128]{1,0:T(8,128)S(1)}, u32[]{:S(2)}, u32[]{:S(2)}) collective-permute-start(f32[32,128]{1,0:T(8,128)S(1)} %shard_map.67), channel_id=1, source_target_pairs={{0,1},{1,0},{2,3},{3,2},{4,5},{5,4},{6,7},{7,6},{8,9},{9,8},{10,11... | collective-permute-start | bytes 49160 | tf_op jit(solution)/shard_map/ppermute | solution.py:287
  56.8 0.8 %collective-permute-done.2.ready = f32[32,128]{1,0:T(8,128)S(1)} collective-permute-done((f32[32,128]{1,0:T(8,128)S(1)}, f32[32,128]{1,0:T(8,128)S(1)}, u32[]{:S(2)}, u32[]{:S(2)}) %collective-permute-start.2) | collective-permute-done | bytes 16416 | tf_op jit(solution)/shard_map/ppermute | solution.py:287
  57.7 8.0 %all_to_all.23 = f32[8,8,128]{2,1,0:T(8,128)S(1)} all-to-all(f32[8,8,128]{2,1,0:T(8,128)S(1)} %shard_map.68), channel_id=1, replica_groups=mesh['x'=4,'z'=8,'y'=4,'c'=2] {'c','y'}, dimensions={0} | all-to-all | bytes 65536 | tf_op jit(solution)/shard_map/all_to_all | solution.py:256
  65.7 0.6 slice_bitcast_fusion
  (4 shorter events, 0.1 us)
Async XLA Ops:
  0.0 8.5 %copy-start = (bf16[4,256,512]{2,1,0:T(8,128)(2,1)S(1)}, bf16[4,256,512]{2,1,0:T(8,128)(2,1)}, u32[]{:S(2)}) copy-start(bf16[4,256,512]{2,1,0:T(8,128)(2,1)} %param.9) | copy-start | bytes 3145732
  0.0 3.5 %copy-start.3 = (bf16[64,1792]{1,0:T(8,128)(2,1)S(1)}, bf16[64,1792]{1,0:T(8,128)(2,1)}, u32[]{:S(2)}) copy-start(bf16[64,1792]{1,0:T(8,128)(2,1)} %param.10) | copy-start | bytes 688132
  0.0 3.5 %copy-start.1 = (bf16[4,256,1792]{2,1,0:T(8,128)(2,1)S(1)}, bf16[4,256,1792]{2,1,0:T(8,128)(2,1)}, u32[]{:S(2)}) copy-start(bf16[4,256,1792]{2,1,0:T(8,128)(2,1)} %param.8) | copy-start | bytes 11010052
  0.0 8.1 %copy-start.2 = (bf16[4,256,512]{2,1,0:T(8,128)(2,1)S(1)}, bf16[4,256,512]{2,1,0:T(8,128)(2,1)}, u32[]{:S(2)}) copy-start(bf16[4,256,512]{2,1,0:T(8,128)(2,1)} %param.7) | copy-start | bytes 3145732
  0.0 8.1 %copy-start.4 = (bf16[64,512]{1,0:T(8,128)(2,1)S(1)}, bf16[64,512]{1,0:T(8,128)(2,1)}, u32[]{:S(2)}) copy-start(bf16[64,512]{1,0:T(8,128)(2,1)} %param.11) | copy-start | bytes 196612
  4.8 4.5 %collective-permute-start = (f32[4,64,256]{2,1,0:T(8,128)S(1)}, f32[4,64,256]{2,1,0:T(8,128)S(1)}, u32[]{:S(2)}, u32[]{:S(2)}) collective-permute-start(f32[4,64,256]{2,1,0:T(8,128)S(1)} %get-tuple-element.10), channel_id=1, source_target_pairs={{0,1},{1,0},{2,3},{3,2},{4,5},{5,4},{6,7},{7,6},{8,9},{9,8},{10,11... | collective-permute-start | bytes 786440 | tf_op jit(solution)/shard_map/ppermute | solution.py:268
  9.0 1.6 %collective-permute-start.1 = (f32[4,64,256]{2,1,0:T(8,128)S(1)}, f32[4,64,256]{2,1,0:T(8,128)S(1)}, u32[]{:S(2)}, u32[]{:S(2)}) collective-permute-start(f32[4,64,256]{2,1,0:T(8,128)S(1)} %get-tuple-element.15), channel_id=1, source_target_pairs={{0,1},{1,0},{2,3},{3,2},{4,5},{5,4},{6,7},{7,6},{8,9},{9,8},{10,11... | collective-permute-start | bytes 786440 | tf_op jit(solution)/shard_map/ppermute | solution.py:271
  55.5 2.1 %collective-permute-start.2 = (f32[32,128]{1,0:T(8,128)S(1)}, f32[32,128]{1,0:T(8,128)S(1)}, u32[]{:S(2)}, u32[]{:S(2)}) collective-permute-start(f32[32,128]{1,0:T(8,128)S(1)} %shard_map.67), channel_id=1, source_target_pairs={{0,1},{1,0},{2,3},{3,2},{4,5},{5,4},{6,7},{7,6},{8,9},{9,8},{10,11... | collective-permute-start | bytes 49160 | tf_op jit(solution)/shard_map/ppermute | solution.py:287

commit v7 on v6

--- a/solution.py
+++ b/solution.py
@@ -76,8 +76,9 @@
         own[...] = pack(low)
         rest = jnp.broadcast_to(diag, (8, LANES))
         for peer in range(send.shape[0]):
-            send[peer, :32] = both
-            send[peer, 32:40] = rest
+            for part in range(8):
+                send[peer, part] = both[4 * part : 4 * part + 4]
+            send[peer, 8] = rest[:4]
 
     @pl.when(lax.axis_index("c") != TRAIN_CORE)
     def _():
@@ -87,8 +88,9 @@
         grad = pack(low)
         own[...] = grad
         for peer in range(send.shape[0]):
-            send[peer, :32] = grad
-            send[peer, 32:40] = grad[:8]
+            for part in range(8):
+                send[peer, part] = grad[4 * part : 4 * part + 4]
+            send[peer, 8] = grad[:4]
 
 
 def spread_kernel(got, own, send):
@@ -98,6 +100,7 @@
         for peer in range(1, got.shape[0]):
             total = total + got[peer]
         grad = own[...]
+        total = jnp.concatenate([total[part] for part in range(9)] + [total[8]], axis=0)
         for peer in range(send.shape[0]):
             send[peer, :40] = total
             send[peer, 40:72] = grad
@@ -106,11 +109,11 @@
     def _():
         for share in range(4):
             for query in range(got.shape[0]):
-                tile = got[query, 8 * share : 8 * share + 8]
+                tile = jnp.concatenate([got[query, 2 * share], got[query, 2 * share + 1]], axis=0)
                 for column in range(4):
                     send[share * 4 + column, 8 * query : 8 * query + 8] = tile
         for peer in range(send.shape[0]):
-            send[peer, 64:72] = got[0, 32:40]
+            send[peer, 64:72] = tile
 
 
 def invert(wide):
@@ -275,7 +278,7 @@
         jnp.concatenate([query_in, query_out], axis=1),
     ) + jnp.concatenate([other_in, other_out], axis=1)
     parts = swap(mine, "y")
-    send, own = call(gram_kernel, (f32(8, 40, LANES), f32(32, LANES)))(parts)
+    send, own = call(gram_kernel, (f32(8, 9, 4, LANES), f32(32, LANES)))(parts)
     got = swap(send, "z")
     send = call(spread_kernel, f32(16, 72, LANES))(got, own)
     got = swap(send, ("y", "x"))

time: 66.5 us -> 66.3 us (level)
  no operation moved by 1% of the time
where the time goes in v7:
time: 66.3 us; the launch traced here: 66.1 us
  blocking collectives  49.9 us (75%)
  matrix products  5.6 us (8%)
  starting transfers between devices  4.69 us (7%)
  Pallas kernels  2.79 us (4%)
  waiting for transfers between devices  2.34 us (4%)
    all_to_all x4, blocking collectives, swap(): return lax.all_to_all(value, axis, 0, 0, tiled=True)  49.9 us
    dot_general x4, matrix products, product(): lax.dot_general(weight, rows, (((1,), (2,)), ((), ())), preferred_element...  5.6 us
    ppermute x1, starting transfers between devices, on_device(): other_in = lax.ppermute(other_in, 'c', flip)  3.32 us
    pallas_call x5, Pallas kernels, wrapped(): pl.pallas_call(body, out_shape=out, in_specs=[VM] * len(args), out_specs=...  2.79 us
    ppermute x1, waiting for transfers between devices, on_device(): lax.ppermute(jnp.where(is_train, query_out, train_out), 'c', flip)  1.35 us
  transfers between devices with their start and end apart: 3, of which 3 were waited for; matrix products, arithmetic and copies ran while one was open for 1% of the time, Pallas kernels for 0%

profile of v7, /device:TPU:1, one launch (start us, length us, event | category | flops | bytes accessed | tf_op | source)
XLA Modules:
  0.0 66.1 jit_solution(12506674548086039673)
XLA Ops:
  0.0 0.0 copy-start
  0.0 0.0 copy-start.3
  0.0 0.0 copy-start.1
  0.0 0.0 copy-start.2
  0.0 0.0 copy-start.4
  0.0 3.5 %convolution_bitcast_fusion.3 = f32[4,64,256]{2,1,0:T(8,128)S(1)} fusion(bf16[4,256,1792]{2,1,0:T(8,128)(2,1)} %param.6, bf16[64,1792]{1,0:T(8,128)(2,1)} %param.10), kind=kOutput, calls=%fused_computation.3 | convolution fusion | flops 234881024 | bytes 4161536 | tf_op jit(solution)/shard_map/dot_general | solution.py:253
  3.5 0.0 copy-done.3
  3.6 0.0 copy-done.1
  3.6 1.2 %broadcast_select_fusion.1 = (f32[4,64,256]{2,1,0:T(8,128)S(1)}, f32[4,64,256]{2,1,0:T(8,128)S(1)}) fusion(f32[4,64,256]{2,1,0:T(8,128)S(1)} %convolution_bitcast_fusion.3, pred[]{:T(512)S(6)} %eq.3, bf16[4,256,1792]{2,1,0:T(8,128)(2,1)S(1)} %copy-done.1, bf16[64,1792]{1,0:T(8,128)(2,1)S(1)} %copy-done.3), kind=kOutput, calls=%fused_computation.9 | convolution fusion | flops 234946560 | bytes 4685825 | tf_op jit(solution)/shard_map/dot_general | solution.py:253
  4.8 3.3 %collective-permute-start = (f32[4,64,256]{2,1,0:T(8,128)S(1)}, f32[4,64,256]{2,1,0:T(8,128)S(1)}, u32[]{:S(2)}, u32[]{:S(2)}) collective-permute-start(f32[4,64,256]{2,1,0:T(8,128)S(1)} %get-tuple-element.10), channel_id=1, source_target_pairs={{0,1},{1,0},{2,3},{3,2},{4,5},{5,4},{6,7},{7,6},{8,9},{9,8},{10,11... | collective-permute-start | bytes 786440 | tf_op jit(solution)/shard_map/ppermute | solution.py:271
  8.1 0.0 copy-done.2
  8.1 0.0 copy-done.4
  8.1 0.4 convolution_bitcast_fusion.1
  8.5 0.0 copy-done
  8.6 0.4 broadcast_select_fusion
  9.0 0.1 collective-permute-start.1
  9.1 0.2 collective-permute-done
  9.3 1.3 %collective-permute-done.1 = f32[4,64,256]{2,1,0:T(8,128)S(1)} collective-permute-done((f32[4,64,256]{2,1,0:T(8,128)S(1)}, f32[4,64,256]{2,1,0:T(8,128)S(1)}, u32[]{:S(2)}, u32[]{:S(2)}) %collective-permute-start.1) | collective-permute-done | bytes 262176 | tf_op jit(solution)/shard_map/ppermute | solution.py:274
  10.6 0.1 fusion
  10.7 11.7 %all_to_all.20.parts = f32[4,128,256]{2,1,0:T(8,128)S(1)} all-to-all(f32[4,128,256]{2,1,0:T(8,128)S(1)} %fusion), channel_id=1, replica_groups=mesh['x'=4,'z'=8,'y'=4,'c'=2] {'y'}, dimensions={0} | all-to-all | bytes 1048576 | tf_op jit(solution)/shard_map/all_to_all | solution.py:259
  22.5 0.4 shard_map.64
  22.9 15.9 %all_to_all.21.got = f32[8,9,4,128]{3,2,1,0:T(4,128)S(1)} all-to-all(f32[8,9,4,128]{3,2,1,0:T(4,128)S(1)} %get-tuple-element.11), channel_id=1, replica_groups=mesh['x'=4,'z'=8,'y'=4,'c'=2] {'z'}, dimensions={0} | all-to-all | bytes 294912 | tf_op jit(solution)/shard_map/all_to_all | solution.py:259
  38.8 14.2 %all_to_all.22.got = f32[16,72,128]{2,1,0:T(8,128)S(1)} all-to-all(f32[16,72,128]{2,1,0:T(8,128)S(1)} %shard_map.65), channel_id=1, replica_groups=mesh['x'=4,'z'=8,'y'=4,'c'=2] {'y','x'}, dimensions={0} | all-to-all | bytes 1179648 | tf_op jit(solution)/shard_map/all_to_all | solution.py:259
  53.1 2.3 %shard_map.67 = f32[32,128]{1,0:T(8,128)S(1)} custom-call(f32[16,72,128]{2,1,0:T(8,128)S(1)} %all_to_all.22.got), custom_call_target="tpu_custom_call" | custom-call | tf_op jit(solution)/shard_map/pallas_call | solution.py:23
  55.4 1.3 %collective-permute-start.2 = (f32[32,128]{1,0:T(8,128)S(1)}, f32[32,128]{1,0:T(8,128)S(1)}, u32[]{:S(2)}, u32[]{:S(2)}) collective-permute-start(f32[32,128]{1,0:T(8,128)S(1)} %shard_map.67), channel_id=1, source_target_pairs={{0,1},{1,0},{2,3},{3,2},{4,5},{5,4},{6,7},{7,6},{8,9},{9,8},{10,11... | collective-permute-start | bytes 49160 | tf_op jit(solution)/shard_map/ppermute | solution.py:290
  56.6 0.8 %collective-permute-done.2.ready = f32[32,128]{1,0:T(8,128)S(1)} collective-permute-done((f32[32,128]{1,0:T(8,128)S(1)}, f32[32,128]{1,0:T(8,128)S(1)}, u32[]{:S(2)}, u32[]{:S(2)}) %collective-permute-start.2) | collective-permute-done | bytes 16416 | tf_op jit(solution)/shard_map/ppermute | solution.py:290
  57.5 8.0 %all_to_all.23 = f32[8,8,128]{2,1,0:T(8,128)S(1)} all-to-all(f32[8,8,128]{2,1,0:T(8,128)S(1)} %shard_map.68), channel_id=1, replica_groups=mesh['x'=4,'z'=8,'y'=4,'c'=2] {'c','y'}, dimensions={0} | all-to-all | bytes 65536 | tf_op jit(solution)/shard_map/all_to_all | solution.py:259
  65.5 0.6 slice_bitcast_fusion
  (4 shorter events, 0.1 us)
Async XLA Ops:
  0.0 8.5 %copy-start = (bf16[4,256,512]{2,1,0:T(8,128)(2,1)S(1)}, bf16[4,256,512]{2,1,0:T(8,128)(2,1)}, u32[]{:S(2)}) copy-start(bf16[4,256,512]{2,1,0:T(8,128)(2,1)} %param.9) | copy-start | bytes 3145732
  0.0 3.5 %copy-start.3 = (bf16[64,1792]{1,0:T(8,128)(2,1)S(1)}, bf16[64,1792]{1,0:T(8,128)(2,1)}, u32[]{:S(2)}) copy-start(bf16[64,1792]{1,0:T(8,128)(2,1)} %param.10) | copy-start | bytes 688132
  0.0 3.5 %copy-start.1 = (bf16[4,256,1792]{2,1,0:T(8,128)(2,1)S(1)}, bf16[4,256,1792]{2,1,0:T(8,128)(2,1)}, u32[]{:S(2)}) copy-start(bf16[4,256,1792]{2,1,0:T(8,128)(2,1)} %param.8) | copy-start | bytes 11010052
  0.0 8.1 %copy-start.2 = (bf16[4,256,512]{2,1,0:T(8,128)(2,1)S(1)}, bf16[4,256,512]{2,1,0:T(8,128)(2,1)}, u32[]{:S(2)}) copy-start(bf16[4,256,512]{2,1,0:T(8,128)(2,1)} %param.7) | copy-start | bytes 3145732
  0.0 8.1 %copy-start.4 = (bf16[64,512]{1,0:T(8,128)(2,1)S(1)}, bf16[64,512]{1,0:T(8,128)(2,1)}, u32[]{:S(2)}) copy-start(bf16[64,512]{1,0:T(8,128)(2,1)} %param.11) | copy-start | bytes 196612
  4.8 4.5 %collective-permute-start = (f32[4,64,256]{2,1,0:T(8,128)S(1)}, f32[4,64,256]{2,1,0:T(8,128)S(1)}, u32[]{:S(2)}, u32[]{:S(2)}) collective-permute-start(f32[4,64,256]{2,1,0:T(8,128)S(1)} %get-tuple-element.10), channel_id=1, source_target_pairs={{0,1},{1,0},{2,3},{3,2},{4,5},{5,4},{6,7},{7,6},{8,9},{9,8},{10,11... | collective-permute-start | bytes 786440 | tf_op jit(solution)/shard_map/ppermute | solution.py:271
  9.0 1.6 %collective-permute-start.1 = (f32[4,64,256]{2,1,0:T(8,128)S(1)}, f32[4,64,256]{2,1,0:T(8,128)S(1)}, u32[]{:S(2)}, u32[]{:S(2)}) collective-permute-start(f32[4,64,256]{2,1,0:T(8,128)S(1)} %get-tuple-element.15), channel_id=1, source_target_pairs={{0,1},{1,0},{2,3},{3,2},{4,5},{5,4},{6,7},{7,6},{8,9},{9,8},{10,11... | collective-permute-start | bytes 786440 | tf_op jit(solution)/shard_map/ppermute | solution.py:274
  55.4 2.1 %collective-permute-start.2 = (f32[32,128]{1,0:T(8,128)S(1)}, f32[32,128]{1,0:T(8,128)S(1)}, u32[]{:S(2)}, u32[]{:S(2)}) collective-permute-start(f32[32,128]{1,0:T(8,128)S(1)} %shard_map.67), channel_id=1, source_target_pairs={{0,1},{1,0},{2,3},{3,2},{4,5},{5,4},{6,7},{7,6},{8,9},{9,8},{10,11... | collective-permute-start | bytes 49160 | tf_op jit(solution)/shard_map/ppermute | solution.py:290
